TPU v7x, 32 devices: a whole 2x2x4 slice. The times are simulated.
32 devices in a mesh: section: 2 (over y), dp: 16 (over z, x, core).
Axes of the slice: x: 2, y: 2, z: 4, core: 2. Of those that a mesh axis runs over, the one named last changes fastest.
Arguments:
- token_ids: int32 [48, 128], P('dp'), may hold values from 0 to 31999
- target_ids: int32 [48, 128], P('dp'), may hold values from 0 to 31999
- time_bins: int32 [48], P('dp'), may hold values from 0 to 127
- sigma_table: float32 [128], replicated, may hold values from 0.2 to 8
- noise: float32 [48, 128, 256], P('dp'), may hold values from -6 to 6
- embed: bfloat16 [32000, 256], P('dp'), may hold values from -6 to 6
- w_in: bfloat16 [256, 1024], replicated, may hold values from -0.375 to 0.375
- w_time: bfloat16 [2, 256, 2048], P('section'), may hold values from -0.375 to 0.375
- norm_gain: float32 [2, 2048], P('section'), may hold values from 0.5 to 1.5
- w_qkv: bfloat16 [2, 1024, 3072], P('section'), may hold values from -0.1875 to 0.1875
- w_out: bfloat16 [2, 1024, 1024], P('section'), may hold values from -0.375 to 0.375
- w_up: bfloat16 [2, 1024, 4096], P('section'), may hold values from -0.1875 to 0.1875
- b_hidden: float32 [2, 4096], P('section'), may hold values from -3 to 3
- w_down: bfloat16 [2, 4096, 1024], P('section'), may hold values from -0.09375 to 0.09375
- out_gain: float32 [1024], replicated, may hold values from 0.5 to 1.5
- head: bfloat16 [32000, 1024], P(('section', 'dp')), may hold values from -0.375 to 0.375
Outputs:
- loss: float32 [], replicated
- grad_embed: float32 [32000, 256], P(('section', 'dp'))
- grad_w_in: float32 [256, 1024], P(('section', 'dp'))
- grad_w_time: float32 [2, 256, 2048], P('section', 'dp')
- grad_norm_gain: float32 [2, 2048], P('section', 'dp')
- grad_w_qkv: float32 [2, 1024, 3072], P('section', 'dp')
- grad_w_out: float32 [2, 1024, 1024], P('section', 'dp')
- grad_w_up: float32 [2, 1024, 4096], P('section', 'dp')
- grad_b_hidden: float32 [2, 4096], P('section', 'dp')
- grad_w_down: float32 [2, 4096, 1024], P('section', 'dp')
- grad_out_gain: float32 [1024], P('dp')
- grad_head: float32 [32000, 1024], P(('section', 'dp'))
All inputs are finite; a program needn't handle non-finite values.
Results may differ from a plain program's by a relative error of at most 0.035.
Values may be sent and summed in bfloat16 or wider, within the bound.
A program may use at most 384 MiB of HBM per device.

v0:
```python
from functools import partial
import math

import jax
import jax.numpy as jnp
from jax import lax
from jax.experimental import pallas as pl
from jax.experimental.pallas import tpu as pltpu
from jax.sharding import Mesh, PartitionSpec as P

HEADS = 16
HEAD_DIM = 64
TFEAT = 256

epsilon = 1e-05
highest = lax.Precision.HIGHEST
f32 = jnp.float32
bf16 = jnp.bfloat16
DP = ("line", "pair", "core")


MESH = pl.DeviceIdType.MESH


def nt(left, right):
    return lax.dot_general(left, right, (((1,), (1,)), ((), ())), preferred_element_type=f32)


def tn(left, right):
    return lax.dot_general(left, right, (((0,), (0,)), ((), ())), preferred_element_type=f32)


def nn(left, right):
    return jnp.dot(left, right, preferred_element_type=f32)


def greet(peers):
    barrier = pltpu.get_barrier_semaphore()
    for peer in peers:
        pl.semaphore_signal(barrier, inc=1, device_id=peer, device_id_type=MESH)
    pl.semaphore_wait(barrier, len(peers))


def remote(source, target, send, recv, peer):
    return pltpu.make_async_remote_copy(
        src_ref=source,
        dst_ref=target,
        send_sem=send,
        recv_sem=recv,
        device_id=peer,
        device_id_type=MESH,
    )


def ring_place(position, line):
    turned = position // line
    return position * (1 - turned) + (2 * line - 1 - position) * turned, turned


def start_kernel(line, *refs):
    ids, embed, head, all_ids, out, head_early, head_core = refs[:7]
    table, found, own, from_core, from_pair, from_line = refs[7:13]
    ids_send, ids_recv, own_sem, core_send, core_recv, pair_send, pair_recv = refs[13:20]
    line_send, line_recv, swap_send, swap_recv, head_send, head_recv = refs[20:]
    me_section = lax.axis_index("section")
    me_line = lax.axis_index("line")
    me_pair = lax.axis_index("pair")
    me_core = lax.axis_index("core")
    section_peer = {"section": 1 - me_section}
    core_peer = {"core": 1 - me_core}
    pair_peer = {"pair": 1 - me_pair}
    peers = []
    for step in range(1, line * 4):
        peers.append(
            {
                "line": lax.rem(me_line + step // 4, line),
                "pair": lax.rem(me_pair + step // 2 % 2, 2),
                "core": lax.rem(me_core + step % 2, 2),
            }
        )
    greet(peers + [section_peer])
    each = head_early.shape[0]
    to_section = remote(
        head.at[pl.ds(0, each)], head_early, head_send.at[0], head_recv.at[0], section_peer
    )
    to_section.start()
    to_other_core = remote(head, head_core, head_send.at[1], head_recv.at[1], core_peer)
    place = all_ids.at[me_line, me_pair, me_core]
    copies = [remote(ids, place, ids_send.at[n], ids_recv.at[n], peer) for n, peer in enumerate(peers)]
    for copy in copies:
        copy.start()
    keep = pltpu.make_async_copy(ids, place, own_sem)
    keep.start()
    rows = embed.shape[0]
    high = table.shape[1]
    half = out.shape[-1]
    padded = jnp.concatenate(
        [embed[...].astype(f32), jnp.zeros((high - rows, embed.shape[1]), f32)], 0
    )
    table[...] = padded.T.astype(bf16)
    keep.wait()
    for copy in copies:
        copy.wait_recv()
    base = ((me_line * 2 + me_pair) * 2 + me_core) * rows

    def pick(spot, pair, core):
        wanted = all_ids[spot, pair, core, pl.ds(me_section, 1), :][:, :half]
        entry = lax.broadcasted_iota(jnp.int32, (high, half), 0)
        entry = jnp.where(entry < rows, entry + base, -1)
        hot = jnp.where(entry == wanted, 1.0, 0.0).astype(bf16)
        return nn(table[...], hot).astype(bf16)

    def core_copy(spot, pair, turn):
        return remote(
            found.at[turn, spot],
            from_core.at[turn, spot],
            core_send.at[turn, spot],
            core_recv.at[turn, spot],
            core_peer,
        )

    def pair_copy(spot):
        return remote(
            from_core.at[0, spot], from_pair.at[spot], pair_send.at[spot], pair_recv.at[spot], pair_peer
        )

    def line_copy(step):
        spot = lax.rem(me_line + step, line)
        return remote(
            from_core.at[1, spot],
            from_line.at[step - 1],
            line_send.at[step - 1],
            line_recv.at[step - 1],
            {"line": spot},
        )

    order = [lax.rem(me_line + step, line) for step in list(range(1, line)) + [0]]
    for turn, pair in enumerate((1 - me_pair, me_pair)):

        @pl.loop(0, line)
        def _(step):
            spot = lax.rem(me_line + 1 + step, line)
            found[turn, spot] = pick(spot, pair, 1 - me_core)
            core_copy(spot, pair, turn).start()
            own[turn, spot] = pick(spot, pair, me_core)

        if turn == 0:
            for spot in order:
                core_copy(spot, pair, 0).wait_recv()
                from_core[0, spot] = from_core[0, spot] + own[0, spot]
                pair_copy(spot).start()
    for step in list(range(1, line)) + [0]:
        spot = lax.rem(me_line + step, line)
        core_copy(spot, me_pair, 1).wait_recv()
        pair_copy(spot).wait_recv()
        from_core[1, spot] = from_core[1, spot] + own[1, spot] + from_pair[spot]
        if step:
            line_copy(step).start()
    to_other_core.start()
    total = from_core[1, me_line]
    for step in range(1, line):
        line_copy(step).wait_recv()
        total = total + from_line[step - 1]
    out[me_section] = total
    swap = remote(out.at[me_section], out.at[me_section], swap_send, swap_recv, section_peer)
    swap.start()
    for copy in copies:
        copy.wait_send()
    for spot in range(line):
        for turn in range(2):
            core_copy(spot, me_pair, turn).wait_send()
        pair_copy(spot).wait_send()
    for step in range(1, line):
        line_copy(step).wait_send()
    swap.wait()
    to_section.wait()
    to_other_core.wait()


def start_pass(ids, embed, head, half, line, collective_id):
    rows, width = embed.shape
    high = -(-rows // 256) * 256
    vmem = pl.BlockSpec(memory_space=pltpu.VMEM)
    anywhere = pl.BlockSpec(memory_space=pl.ANY)
    dma = pltpu.SemaphoreType.DMA
    block = (width, half)
    return pl.pallas_call(
        partial(start_kernel, line),
        out_shape=[
            jax.ShapeDtypeStruct((line, 2, 2) + ids.shape, ids.dtype),
            jax.ShapeDtypeStruct((2,) + block, bf16),
            jax.ShapeDtypeStruct((head.shape[0] // 8 * 5, head.shape[1]), bf16),
            jax.ShapeDtypeStruct(head.shape, bf16),
        ],
        in_specs=[vmem, vmem, anywhere],
        out_specs=[vmem, vmem, anywhere, anywhere],
        scratch_shapes=[
            pltpu.VMEM((width, high), bf16),
            pltpu.VMEM((2, line) + block, bf16),
            pltpu.VMEM((2, line) + block, bf16),
            pltpu.VMEM((2, line) + block, bf16),
            pltpu.VMEM((line,) + block, bf16),
            pltpu.VMEM((line - 1,) + block, bf16),
            dma((line * 4 - 1,)),
            dma((line * 4 - 1,)),
            dma,
            dma((2, line)),
            dma((2, line)),
            dma((line,)),
            dma((line,)),
            dma((line - 1,)),
            dma((line - 1,)),
            dma,
            dma,
            dma((2,)),
            dma((2,)),
        ],
        compiler_params=pltpu.CompilerParams(
            collective_id=collective_id, has_side_effects=True, vmem_limit_bytes=40 * 2**20
        ),
        cost_estimate=pl.CostEstimate(flops=0, bytes_accessed=2**27, transcendentals=0),
    )(ids, embed, head)


def head_kernel(line, head_rows, length, *refs):
    final, targets, *heads = refs[:7]
    out, grads, lse_out, pick_out = refs[7:11]
    (table, rows_all, logits, probs, acc, parts, from_pair, from_line, stats, done) = refs[11:21]
    (head_sem, own_sem, give_send, give_recv, along_send, along_recv, pair_send, pair_recv) = refs[21:29]
    (stat_send, stat_recv, sum_send, sum_recv, line_send, line_recv, back_send, back_recv) = refs[29:37]
    last_send, last_recv = refs[37:]
    half = final.shape[0] // 2
    width = 2 * half
    padded = heads[0].shape[0]
    me_section = lax.axis_index("section")
    me_line = lax.axis_index("line")
    me_pair = lax.axis_index("pair")
    me_core = lax.axis_index("core")
    section_peer = {"section": 1 - me_section}
    pair_peer = {"pair": 1 - me_pair}
    chip_peers = []
    for step in range(1, 2 * line):
        chip_peers.append(
            {"line": lax.rem(me_line + step // 2, line), "pair": lax.rem(me_pair + step % 2, 2)}
        )
    greet(chip_peers + [section_peer, {"core": 1 - me_core}])

    def side(pair):
        return pl.ds(pl.multiple_of(pair * half, 16), half)

    loads = []
    for n, part in enumerate(heads):
        first = sum(other.shape[0] for other in heads[:n])
        target = table.at[pl.ds(first, part.shape[0])]
        loads.append(pltpu.make_async_copy(part, target, head_sem.at[n]))
    late = heads[3]
    last = remote(
        late,
        table.at[pl.ds(4 * padded - late.shape[0], late.shape[0])],
        last_send,
        last_recv,
        {"core": 1 - me_core},
    )
    last.start()
    for load in loads:
        load.start()

    quarter = half // 2

    def token_rows(place, pair, chunk):
        first = place * width + pair * half + chunk * quarter
        return pl.ds(pl.multiple_of(first, 16), quarter)

    def group(place):
        return pl.ds(pl.multiple_of(place * width, 128), width)

    def column_block(place, chunk):
        return rows_all.at[token_rows(place, me_pair, chunk)]

    def give(chunk):
        return remote(
            final.at[pl.ds(chunk * quarter, quarter)],
            column_block(me_line, chunk),
            give_send.at[chunk],
            give_recv.at[chunk],
            section_peer,
        )

    def along(step, way, chunk):
        block = column_block(me_line - way * step, chunk)
        turn = (way + 1) // 2
        return remote(
            block,
            block,
            along_send.at[turn, step, chunk],
            along_recv.at[turn, step, chunk],
            {"line": me_line + way},
        )

    def inside(place):
        return (place >= 0) & (place < line)

    def sends_along(step, way):
        return inside(me_line - way * step) & inside(me_line + way)

    def sideways(place, chunk):
        block = column_block(place, chunk)
        return remote(
            block, block, pair_send.at[place, chunk], pair_recv.at[place, chunk], pair_peer
        )

    def arrived_sideways(place, chunk):
        block = rows_all.at[token_rows(place, 1 - me_pair, chunk)]
        return remote(
            block, block, pair_send.at[place, chunk], pair_recv.at[place, chunk], pair_peer
        )

    @pl.when(me_section == 1)
    def _():
        for chunk in range(2):
            give(chunk).start()
        for chunk in range(2):
            keep = pltpu.make_async_copy(
                final.at[pl.ds(half + chunk * quarter, quarter)],
                column_block(me_line, chunk),
                own_sem.at[chunk],
            )
            keep.start()
            keep.wait()

    for chunk in range(2):

        @pl.when(me_section == 0)
        def _():
            give(chunk).wait_recv()

        for way in (1, -1):

            @pl.when(sends_along(0, way))
            def _():
                along(0, way, chunk).start()

        sideways(me_line, chunk).start()

    def pass_on(step):
        for chunk in range(2):
            for way in (1, -1):
                place = me_line - way * step

                @pl.when(inside(place))
                def _():
                    block = column_block(place, chunk)
                    turn = (way + 1) // 2
                    remote(
                        block,
                        block,
                        along_send.at[turn, step - 1, chunk],
                        along_recv.at[turn, step - 1, chunk],
                        {"line": me_line - way},
                    ).wait_recv()

                    @pl.when(inside(me_line + way))
                    def _():
                        along(step, way, chunk).start()

                    sideways(place, chunk).start()

    nearest = []
    for own in range(line):
        near = [own]
        for step in range(1, line):
            near += [place for place in (own - step, own + step) if 0 <= place < line]
        nearest.append(near)

    def by_distance(turn):
        place = 0
        for own in range(line):
            for n in range(line):
                hit = ((me_line == own) & (turn == n)).astype(jnp.int32)
                place = place + hit * nearest[own][n]
        return place

    def vocabulary(tile, rows):
        shard = tile * rows // padded
        first = lax.rem(tile * rows, padded)
        shard_section = lax.rem(me_section + shard // 2, 2)
        shard_core = lax.rem(me_core + lax.rem(shard, 2), 2)
        base = (((shard_section * line + me_line) * 2 + me_pair) * 2 + shard_core) * head_rows
        row = lax.broadcasted_iota(jnp.int32, (rows, 1), 0) + first
        return jnp.where(row < head_rows, row + base, -1)

    tile_rows = 512
    tiles = 4 * padded // tile_rows
    lowest = -1e30

    def score(turn, tops):
        place = by_distance(turn) if turn < line else None
        before = by_distance(turn - 1) if turn > 0 else None
        wanted = None if place is None else targets[place]

        def one(tile, carry):
            rows = pl.ds(pl.multiple_of(tile * tile_rows, tile_rows), tile_rows)
            out = []
            if place is not None:
                top, pick = carry[:2]
                entry = vocabulary(tile, tile_rows)
                part = nt(table[rows, :], rows_all[group(place), :])
                part = jnp.where(entry >= 0, part, lowest)
                logits[turn % 2, rows, :] = part
                out.append(jnp.maximum(top, jnp.max(part, 0, keepdims=True)))
                out.append(
                    pick + jnp.sum(jnp.where(entry == wanted, part, 0.0), 0, keepdims=True)
                )
            if before is not None:
                value = jnp.exp(logits[(turn - 1) % 2, rows, :] - tops)
                probs[rows, group(before)] = value.astype(bf16)
                out.append(carry[-1] + jnp.sum(value, 0, keepdims=True))
            return tuple(out)

        none = jnp.zeros((1, width), f32)
        start = () if place is None else (jnp.full((1, width), lowest, f32), none)
        start += () if before is None else (none,)
        result = lax.fori_loop(0, tiles, one, start)
        if place is not None:
            pick_out[place] = result[1]
        if before is not None:
            own = stats.at[me_line, me_pair, before]
            own[:, 0:width] = tops
            own[:, width : 2 * width] = result[-1]
            for n in range(len(chip_peers)):
                stat_copy(n, before).start()
        return None if place is None else result[0]

    def stat_copy(n, place):
        own = stats.at[me_line, me_pair, place]
        return remote(own, own, stat_send.at[n, place], stat_recv.at[n, place], chip_peers[n])

    def stat_wait(n, place):
        peer = chip_peers[n]
        source_line = lax.rem(2 * me_line + line - peer["line"], line)
        source_pair = peer["pair"]
        block = stats.at[source_line, source_pair, place]
        remote(block, block, stat_send.at[n, place], stat_recv.at[n, place], peer).wait_recv()

    for load in loads:
        load.wait()
    last.wait()

    tops = None
    for turn in range(line + 1):
        if turn + 1 < line:
            pass_on(turn + 1)
        if turn < line:
            for chunk in range(2):
                arrived_sideways(by_distance(turn), chunk).wait_recv()
        tops = score(turn, tops)

    def part_rows(pair, chunk):
        return pl.ds(pl.multiple_of(pair * half + chunk * quarter, 16), quarter)

    def sum_copy(turn, chunk):
        place = lax.rem(me_line + turn + 1, line)
        return remote(
            parts.at[place, part_rows(1 - me_pair, chunk)],
            from_pair.at[turn, pl.ds(chunk * quarter, quarter)],
            sum_send.at[turn, chunk],
            sum_recv.at[turn, chunk],
            pair_peer,
        )

    def line_copy(turn, chunk):
        place = lax.rem(me_line + turn + 1, line)
        return remote(
            parts.at[place, part_rows(me_pair, chunk)],
            from_line.at[turn, pl.ds(chunk * quarter, quarter)],
            line_send.at[turn, chunk],
            line_recv.at[turn, chunk],
            {"line": place},
        )

    def finish(turn, chunk):
        place = lax.rem(me_line + turn + 1, line)
        sum_copy(turn, chunk).wait_recv()
        own = parts.at[place, part_rows(me_pair, chunk)]
        other = from_pair.at[turn, pl.ds(chunk * quarter, quarter)]

        @pl.loop(0, quarter // 16)
        def _(block):
            rows = pl.ds(pl.multiple_of(block * 16, 16), 16)
            own[rows, :] = (own[rows, :].astype(f32) + other[rows, :].astype(f32)).astype(bf16)

    @pl.loop(0, line)
    def _(turn):
        place = lax.rem(me_line + turn + 1, line)
        for n in range(len(chip_peers)):
            stat_wait(n, place)
        tops = [stats[a, b, place, :, 0:width] for a in range(line) for b in range(2)]
        totals = [
            stats[a, b, place, :, width : 2 * width] for a in range(line) for b in range(2)
        ]
        top = tops[0]
        for value in tops[1:]:
            top = jnp.maximum(top, value)
        total = jnp.zeros_like(top)
        for peak, part in zip(tops, totals):
            total = total + part * jnp.exp(peak - top)
        lse = top + jnp.log(total)
        lse_out[place] = lse
        factor = jnp.exp(stats[me_line, me_pair, place, :, 0:width] - lse) / length
        wanted = targets[place]

        def scaled(tile):
            rows = pl.ds(tile * padded, padded)
            entry = vocabulary(tile, padded)
            grad = probs[rows, group(place)].astype(f32) * factor
            grad = (grad - jnp.where(entry == wanted, 1.0 / length, 0.0)).astype(bf16)
            probs[rows, group(place)] = grad
            return grad

        grad = scaled(0)
        for tile in range(4):
            product = tn(grad, table[pl.ds(tile * padded, padded), :])
            if tile < 3:
                grad = scaled(tile + 1)
                acc[...] = product if tile == 0 else acc[...] + product
            else:
                parts[place] = (acc[...] + product).astype(bf16)

        for chunk in range(2):
            sum_copy(turn, chunk).start()

        @pl.when(turn > 0)
        def _():
            for chunk in range(2):
                finish(turn - 1, chunk)
                line_copy(turn - 1, chunk).start()

    gh_rows = 256
    gh_tiles = 4 * padded // gh_rows

    def head_grads(first, last):
        @pl.loop(first, last)
        def _(tile):
            rows = pl.ds(pl.multiple_of(tile * gh_rows, gh_rows), gh_rows)
            value = jnp.dot(probs[rows, :], rows_all[...], preferred_element_type=f32)
            grads[rows, :] = value.astype(bf16)

    def back(chunk):
        part = pl.ds(chunk * quarter, quarter)
        return remote(
            done.at[part], out.at[part], back_send.at[chunk], back_recv.at[chunk], section_peer
        )

    head_grads(0, gh_tiles // 2)
    for chunk in range(2):
        finish(line - 1, chunk)
        for turn in range(line - 1):
            line_copy(turn, chunk).wait_recv()
        own = parts.at[me_line, part_rows(me_pair, chunk)]

        @pl.loop(0, quarter // 16)
        def _(block):
            rows = pl.ds(pl.multiple_of(block * 16, 16), 16)
            chunk_rows = pl.ds(pl.multiple_of(chunk * quarter + block * 16, 16), 16)
            value = own[rows, :].astype(f32)
            for turn in range(line - 1):
                value = value + from_line[turn, chunk_rows, :].astype(f32)
            done[chunk_rows, :] = value.astype(bf16)

        @pl.when(me_section == 0)
        def _():
            back(chunk).start()

    @pl.when(me_section == 0)
    def _():
        out[...] = jnp.zeros_like(out)

    @pl.when(me_section == 1)
    def _():
        out[pl.ds(half, half), :] = done[...]

    head_grads(gh_tiles // 2, gh_tiles)
    for chunk in range(2):

        @pl.when(me_section == 0)
        def _():
            back(chunk).wait_send()

        @pl.when(me_section == 1)
        def _():
            back(chunk).wait_recv()
            give(chunk).wait_send()

        for way in (1, -1):
            for step in range(line - 1):

                @pl.when(sends_along(step, way))
                def _():
                    along(step, way, chunk).wait_send()

        for place in range(line):
            sideways(place, chunk).wait_send()
        for turn in range(line):
            sum_copy(turn, chunk).wait_send()
        for turn in range(line - 1):
            line_copy(turn, chunk).wait_send()
    for place in range(line):
        for n in range(len(chip_peers)):
            stat_copy(n, place).wait_send()


def head_pass(final, targets, heads, line, head_rows, length, collective_id):
    tokens, deep = final.shape
    half = tokens // 2
    padded = heads[0].shape[0]
    vmem = pl.BlockSpec(memory_space=pltpu.VMEM)
    anywhere = pl.BlockSpec(memory_space=pl.ANY)
    dma = pltpu.SemaphoreType.DMA
    peers = 2 * line - 1
    return pl.pallas_call(
        partial(head_kernel, line, head_rows, length),
        out_shape=[
            jax.ShapeDtypeStruct((tokens, deep), bf16),
            jax.ShapeDtypeStruct((4 * padded, deep), bf16),
            jax.ShapeDtypeStruct((line, 1, tokens), f32),
            jax.ShapeDtypeStruct((line, 1, tokens), f32),
        ],
        in_specs=[vmem, vmem] + [anywhere] * len(heads),
        out_specs=[vmem] * 4,
        scratch_shapes=[
            pltpu.VMEM((4 * padded, deep), bf16),
            pltpu.VMEM((line * tokens, deep), bf16),
            pltpu.VMEM((2, 4 * padded, tokens), f32),
            pltpu.VMEM((4 * padded, line * tokens), bf16),
            pltpu.VMEM((tokens, deep), f32),
            pltpu.VMEM((line, tokens, deep), bf16),
            pltpu.VMEM((line, half, deep), bf16),
            pltpu.VMEM((line - 1, half, deep), bf16),
            pltpu.VMEM((line, 2, line, 1, 2 * tokens), f32),
            pltpu.VMEM((half, deep), bf16),
            dma((len(heads),)),
            dma((2,)),
            dma((2,)),
            dma((2,)),
            dma((2, line, 2)),
            dma((2, line, 2)),
            dma((line, 2)),
            dma((line, 2)),
            dma((peers, line)),
            dma((peers, line)),
            dma((line, 2)),
            dma((line, 2)),
            dma((line, 2)),
            dma((line, 2)),
            dma((2,)),
            dma((2,)),
            dma,
            dma,
        ],
        compiler_params=pltpu.CompilerParams(
            collective_id=collective_id, has_side_effects=True, vmem_limit_bytes=60 * 2**20
        ),
        cost_estimate=pl.CostEstimate(
            flops=24 * line * padded * tokens * deep, bytes_accessed=2**28, transcendentals=0
        ),
    )(final, targets, *heads)


def row_stats(values):
    centred = values - jnp.mean(values, -1, keepdims=True)
    factor = lax.rsqrt(jnp.mean(centred * centred, -1, keepdims=True) + epsilon)
    return centred * factor, factor


def two_heads(block):
    first = lax.broadcasted_iota(jnp.int32, block.shape, 1) < HEAD_DIM
    zero = jnp.zeros_like(block)
    return jnp.concatenate([jnp.where(first, block, zero), jnp.where(first, zero, block)], 0)


def one_block(stacked):
    rows = stacked.shape[0] // 2
    first = lax.broadcasted_iota(jnp.int32, (rows, stacked.shape[1]), 1) < HEAD_DIM
    return jnp.where(first, stacked[:rows], stacked[rows:])


def attention_weights(queries, keys):
    scores = nt(keys, queries) * (1.0 / math.sqrt(HEAD_DIM))
    exped = jnp.exp(scores - jnp.max(scores, 0, keepdims=True))
    return exped * (1.0 / jnp.sum(exped, 0, keepdims=True))


def tile_of(index, size):
    return pl.ds(pl.multiple_of(index * size, size), size)


def forward_kernel(seqs, *refs):
    refs = list(refs)

    def take(number):
        return [refs.pop(0) for _ in range(number)]

    start, scale, bias, gain = take(4)
    weights = take(4)
    head, head_early = take(2)
    out, final, x, joined, mixed, middle, entry_attn, entry_mlp, slope, hidden = take(10)
    head_late, head_fourth = take(2)
    w_qkv, w_out, w_up, w_down, x_total, arrived, sems, relay_send, relay_recv = take(9)
    head_send, head_recv = refs
    width = start.shape[1]
    length = start.shape[0] // seqs
    me_section = lax.axis_index("section")
    section_peer = {"section": 1 - me_section}
    load_qkv, load_out, load_up, load_down = [
        pltpu.make_async_copy(source.at[0], target, sems.at[n])
        for n, (source, target) in enumerate(zip(weights, (w_qkv, w_out, w_up, w_down)))
    ]
    load_qkv.start()
    core_peer = {"core": 1 - lax.axis_index("core")}
    greet([section_peer, core_peer])
    each = head_early.shape[0]
    to_section = remote(
        head.at[pl.ds(each, head_late.shape[0])],
        head_late,
        head_send.at[0],
        head_recv.at[0],
        section_peer,
    )
    to_section.start()
    to_core = remote(head_early, head_fourth, head_send.at[1], head_recv.at[1], core_peer)
    to_core.start()

    def relay(seq):
        rows = pl.ds(seq * length, length)
        return remote(
            out.at[rows], arrived.at[rows], relay_send.at[seq], relay_recv.at[seq], section_peer
        )

    tile = 512

    def enter(seq):
        rows = pl.ds(seq * length, length)

        @pl.when(me_section == 0)
        def _():
            x[rows, :] = start[rows, :]

        @pl.when(me_section == 1)
        def _():
            relay(seq).wait_recv()
            x[rows, :] = arrived[rows, :].astype(f32)

        normed, _ = row_stats(x[rows, :])
        entry_attn[rows, :] = (normed * scale[seq, :, :width]).astype(bf16)

    def join(first, count):
        rows = pl.ds(first * length, count * length)

        @pl.loop(0, 3 * width // tile)
        def _(index):
            cols = tile_of(index, tile)
            joined[rows, cols] = nn(entry_attn[rows, :], w_qkv[:, cols]).astype(bf16)

    for seq in range(seqs - 1):
        enter(seq)
    load_qkv.wait()
    load_out.start()
    load_up.start()
    join(0, seqs - 1)
    enter(seqs - 1)
    join(seqs - 1, 1)
    load_out.wait()
    load_down.start()
    pairs = width // 128

    @pl.loop(0, pairs)
    def _(pair):
        cols = tile_of(pair, 128)
        for seq in range(seqs):
            rows = pl.ds(seq * length, length)
            queries = two_heads(joined[rows, cols])
            keys = joined[rows, tile_of(pair + pairs, 128)]
            values = joined[rows, tile_of(pair + 2 * pairs, 128)]
            probs = attention_weights(queries, keys).astype(bf16)
            mixed[rows, cols] = one_block(tn(probs, values)).astype(bf16)

    @pl.loop(0, width // tile)
    def _(index):
        cols = tile_of(index, tile)
        middle[:, cols] = x[:, cols] + nn(mixed[...], w_out[:, cols])

    for seq in range(seqs):
        rows = pl.ds(seq * length, length)
        normed, _ = row_stats(middle[rows, :])
        entry_mlp[rows, :] = (normed * scale[seq, :, width:]).astype(bf16)

    load_up.wait()
    load_down.wait()

    def gelu_of(up, rows, cols):
        below = 0.5 + 0.5 * lax.erf(up * math.sqrt(0.5))
        value = (up * below).astype(bf16)
        density = jnp.exp(-0.5 * up * up) * (1.0 / math.sqrt(2.0 * math.pi))
        slope[rows, cols] = (below + up * density).astype(bf16)
        hidden[rows, cols] = value
        return value

    def feed_forward(first, count):
        rows = pl.ds(first * length, count * length)

        def one(index, total):
            sides = [tile_of(2 * index + side, tile) for side in range(2)]
            ups = [nn(entry_mlp[rows, :], w_up[:, cols]) + bias[:, cols] for cols in sides]
            both = jnp.concatenate([gelu_of(up, rows, cols) for up, cols in zip(ups, sides)], 1)
            x_total[rows, :] += nn(both, w_down[tile_of(index, 2 * tile), :])
            return total

        x_total[rows, :] = middle[rows, :]
        lax.fori_loop(0, w_up.shape[1] // (2 * tile), one, 0)
        for seq in range(first, first + count):
            rows = pl.ds(seq * length, length)
            value = x_total[rows, :].astype(bf16)
            out[rows, :] = value

            @pl.when(me_section == 0)
            def _():
                relay(seq).start()

            normed, _ = row_stats(value.astype(f32))
            final[rows, :] = (normed * gain[...]).astype(bf16)

    feed_forward(0, seqs)

    to_section.wait()
    to_core.wait()

    @pl.when(me_section == 0)
    def _():
        for seq in range(seqs):
            relay(seq).wait_send()


def layer_scratch(width, hidden):
    return [
        pltpu.VMEM((width, 3 * width), bf16),
        pltpu.VMEM((width, width), bf16),
        pltpu.VMEM((width, hidden), bf16),
        pltpu.VMEM((hidden, width), bf16),
    ]


def forward_pass(start, scale, weights, gain, head, head_early, collective_id):
    w_qkv, w_out, w_up, b_hidden, w_down = weights
    tokens, width = start.shape
    wide = w_up.shape[-1]
    seqs = scale.shape[0]
    vmem = pl.BlockSpec(memory_space=pltpu.VMEM)
    anywhere = pl.BlockSpec(memory_space=pl.ANY)

    def low(columns):
        return (tokens, columns), bf16

    exact = ((tokens, width), f32)
    results = [low(width), low(width), exact, low(3 * width), low(width), exact, low(width)]
    results += [low(width), low(wide), low(wide)]
    results += [((head.shape[0] - head_early.shape[0], width), bf16), (head_early.shape, bf16)]
    scratch = layer_scratch(width, wide) + [pltpu.VMEM(*exact), pltpu.VMEM(*low(width))]
    dma = pltpu.SemaphoreType.DMA
    flops = 4 * tokens * (4 * width * width + 2 * width * wide)
    return pl.pallas_call(
        partial(forward_kernel, seqs),
        out_shape=[jax.ShapeDtypeStruct(*item) for item in results],
        in_specs=[vmem] * 4 + [anywhere] * 6,
        out_specs=[vmem] * (len(results) - 2) + [anywhere] * 2,
        scratch_shapes=scratch + [dma((4,)), dma((seqs,)), dma((seqs,)), dma((2,)), dma((2,))],
        compiler_params=pltpu.CompilerParams(
            collective_id=collective_id, has_side_effects=True, vmem_limit_bytes=60 * 2**20
        ),
        cost_estimate=pl.CostEstimate(flops=2 * flops, bytes_accessed=2**25, transcendentals=0),
    )(start, scale, b_hidden, gain, w_qkv, w_out, w_up, w_down, head, head_early)


def norm_grads(source, total, grad_middle, scale, grad_cond, half, seq, store):
    width = total.shape[1]
    length = total.shape[0] // scale.shape[0]
    rows = pl.ds(seq * length, length)
    cols = pl.ds(half * width, width)
    normed, factor = row_stats(source[rows, :])
    gradient = total[rows, :]
    if grad_cond is not None:
        grad_cond[seq, :, cols] = jnp.sum(gradient * normed, 0, keepdims=True)
    scaled = gradient * scale[seq, :, cols]
    back = factor * (
        scaled
        - jnp.mean(scaled, -1, keepdims=True)
        - normed * jnp.mean(scaled * normed, -1, keepdims=True)
    )
    store(rows, grad_middle[rows, :] + back)


def attention_grads(joined, grad_mixed, grad_joined, pair, seqs):
    pairs = grad_mixed.shape[1] // 128
    length = grad_mixed.shape[0] // seqs
    shrink = 1.0 / math.sqrt(HEAD_DIM)
    cols = tile_of(pair, 128)
    key_cols = tile_of(pair + pairs, 128)
    value_cols = tile_of(pair + 2 * pairs, 128)
    for seq in range(seqs):
        rows = pl.ds(seq * length, length)
        queries = two_heads(joined[rows, cols])
        keys = joined[rows, key_cols]
        probs = attention_weights(queries, keys)
        grads = two_heads(grad_mixed[rows, cols])
        grad_probs = nt(joined[rows, value_cols], grads)
        inner = jnp.sum(grad_probs * probs, 0, keepdims=True)
        grad_scores = (probs * (grad_probs - inner)).astype(bf16)
        grad_joined[rows, cols] = (one_block(tn(grad_scores, keys)) * shrink).astype(bf16)
        grad_joined[rows, key_cols] = (nn(grad_scores, queries) * shrink).astype(bf16)
        grad_joined[rows, value_cols] = nn(probs.astype(bf16), grads).astype(bf16)


def backward_kernel(begin, seqs, *refs):
    refs = list(refs)

    def take(number):
        return [refs.pop(0) for _ in range(number)]

    if begin:
        incoming, other, hidden, entry = take(4)
        far = take(3)
        grad_middle, total, grad_bias, down_out, up_out = take(5)
        grad_low, grad_up, entry_turned, down_weight, up_weight, out_sem = take(6)
        near = take(3)
    else:
        scale, incoming, other, gain = take(4)
        far = take(8)
        out, grad_top, grad_gain = take(3)
        grad_low, grad_up, grad_attn, grad_joined = take(4)
        near = take(8)
        total, grad_middle, grad_mixed = take(3)
    (sems,) = refs
    if begin:
        slope, w_up, w_down = near
        load_slope = pltpu.make_async_copy(far[0], slope, sems.at[0])
        load_up = pltpu.make_async_copy(far[1].at[0], w_up, sems.at[1])
        load_down = pltpu.make_async_copy(far[2].at[0], w_down, sems.at[2])
    else:
        slope, w_up, w_down, x, middle, joined, w_qkv, w_out = near
        load_slope = pltpu.make_async_copy(far[0], slope, sems.at[0])
        load_up = pltpu.make_async_copy(far[1].at[0], w_up, sems.at[1])
        load_down = pltpu.make_async_copy(far[2].at[0], w_down, sems.at[2])
        load_x = pltpu.make_async_copy(far[3], x, sems.at[3])
        load_middle = pltpu.make_async_copy(far[4], middle, sems.at[4])
        load_joined = pltpu.make_async_copy(far[5], joined, sems.at[5])
        load_qkv = pltpu.make_async_copy(far[6].at[0], w_qkv, sems.at[6])
        load_out = pltpu.make_async_copy(far[7].at[0], w_out, sems.at[7])
    width = incoming.shape[1]
    length = incoming.shape[0] // seqs
    load_down.start()
    load_slope.start()
    if begin:
        entry_turned[...] = entry[...].T

    for seq in range(seqs):
        rows = pl.ds(seq * length, length)
        if begin:
            first = (lax.axis_index("section") == 0).astype(f32)
            value = incoming[rows, :].astype(f32) * first + other[rows, :] * (1.0 - first)
        else:
            normed, factor = row_stats(other[rows, :].astype(f32))
            gradient = incoming[rows, :].astype(f32)
            part = jnp.sum(gradient * normed, 0, keepdims=True)
            grad_gain[...] = part if seq == 0 else grad_gain[...] + part
            scaled = gradient * gain[...]
            value = factor * (
                scaled
                - jnp.mean(scaled, -1, keepdims=True)
                - normed * jnp.mean(scaled * normed, -1, keepdims=True)
            )
            grad_top[rows, :] = value
        grad_middle[rows, :] = value
        grad_low[rows, :] = value.astype(bf16)

    load_down.wait()
    load_slope.wait()
    load_up.start()
    if not begin:
        load_middle.start()
        load_out.start()
        load_joined.start()
    tile = 1024

    @pl.loop(0, w_up.shape[1] // tile)
    def _(index):
        cols = tile_of(index, tile)
        grad_hidden = nt(grad_low[...], w_down[cols, :])
        value = (grad_hidden * slope[:, cols].astype(f32)).astype(bf16)
        grad_up[:, cols] = value
        if begin:
            grad_bias[:, cols] = jnp.sum(value.astype(f32), 0, keepdims=True)
            down_weight[cols, :] = tn(hidden[:, cols], grad_low[...]).astype(bf16)
            pltpu.make_async_copy(
                down_weight.at[cols], down_out.at[cols], out_sem.at[0, index]
            ).start()
            up_weight[:, cols] = nn(entry_turned[...], value).astype(bf16)

    if begin:
        whole_up = pltpu.make_async_copy(up_weight, up_out, out_sem.at[1, 0])
        whole_up.start()
    load_up.wait()
    if not begin:
        load_middle.wait()
        load_out.wait()
        load_joined.wait()
        load_qkv.start()
        load_x.start()

    @pl.loop(0, width // 256)
    def _(index):
        total[:, tile_of(index, 256)] = nt(grad_up[...], w_up[tile_of(index, 256), :])

    if begin:
        for index in range(w_up.shape[1] // tile):
            cols = pl.ds(index * tile, tile)
            pltpu.make_async_copy(
                down_weight.at[cols], down_out.at[cols], out_sem.at[0, index]
            ).wait()
        whole_up.wait()
        return

    def store_middle(rows, value):
        grad_middle[rows, :] = value
        grad_attn[rows, :] = value.astype(bf16)

    for seq in range(seqs):
        norm_grads(middle, total, grad_middle, scale, None, 1, seq, store_middle)

    @pl.loop(0, width // 512)
    def _(index):
        part = tile_of(index, 512)
        grad_mixed[:, part] = nt(grad_attn[...], w_out[part, :]).astype(bf16)

    @pl.loop(0, width // 128)
    def _(pair):
        attention_grads(joined, grad_mixed, grad_joined, pair, seqs)

    load_qkv.wait()
    load_x.wait()

    @pl.loop(0, width // 256)
    def _(index):
        total[:, tile_of(index, 256)] = nt(grad_joined[...], w_qkv[tile_of(index, 256), :])

    def store_out(rows, value):
        out[rows, :] = value.astype(bf16)

    for seq in range(seqs):
        norm_grads(x, total, grad_middle, scale, None, 0, seq, store_out)


def backward_pass(grad_final, block_out, gain, scale, kept, weights):
    w_qkv, w_out, w_up, _, w_down = weights
    x, joined, _, middle, _, _, slope, _ = kept
    tokens, width = x.shape
    wide = w_up.shape[-1]
    vmem = pl.BlockSpec(memory_space=pltpu.VMEM)
    anywhere = pl.BlockSpec(memory_space=pl.ANY)
    exact = ((tokens, width), f32)
    low = ((tokens, width), bf16)
    lows = [low, ((tokens, wide), bf16), low, ((tokens, 3 * width), bf16)]
    near = [
        ((tokens, wide), bf16),
        ((width, wide), bf16),
        ((wide, width), bf16),
        exact,
        exact,
        ((tokens, 3 * width), bf16),
        ((width, 3 * width), bf16),
        ((width, width), bf16),
    ]
    flops = 4 * tokens * (4 * width * width + 2 * width * wide)
    return pl.pallas_call(
        partial(backward_kernel, False, scale.shape[0]),
        out_shape=[jax.ShapeDtypeStruct(*item) for item in [low, exact, ((1, width), f32)]],
        in_specs=[vmem] * 4 + [anywhere] * 8,
        out_specs=[vmem] * 3,
        scratch_shapes=[pltpu.VMEM(*item) for item in lows + near + [exact, exact, low]]
        + [pltpu.SemaphoreType.DMA((8,))],
        compiler_params=pltpu.CompilerParams(vmem_limit_bytes=60 * 2**20),
        cost_estimate=pl.CostEstimate(flops=flops, bytes_accessed=2**25, transcendentals=0),
    )(scale, grad_final, block_out, gain, slope, w_up, w_down, x, middle, joined, w_qkv, w_out)


def backward_begin(returned, grad_top, seqs, hidden, entry, slope, w_up, w_down):
    tokens, width = grad_top.shape
    wide = w_up.shape[-1]
    vmem = pl.BlockSpec(memory_space=pltpu.VMEM)
    anywhere = pl.BlockSpec(memory_space=pl.ANY)
    exact = ((tokens, width), f32)
    low = ((tokens, width), bf16)
    wide_low = ((tokens, wide), bf16)
    up, down = ((width, wide), bf16), ((wide, width), bf16)
    results = [exact, exact, ((1, wide), f32), down, up]
    inside = [low, wide_low, ((width, tokens), bf16), down, up]
    return pl.pallas_call(
        partial(backward_kernel, True, seqs),
        out_shape=[jax.ShapeDtypeStruct(*item) for item in results],
        in_specs=[vmem] * 4 + [anywhere] * 3,
        out_specs=[vmem] * 3 + [anywhere] * 2,
        scratch_shapes=[pltpu.VMEM(*item) for item in inside]
        + [pltpu.SemaphoreType.DMA((2, wide // 1024))]
        + [pltpu.VMEM(*item) for item in (wide_low, up, down)]
        + [pltpu.SemaphoreType.DMA((3,))],
        compiler_params=pltpu.CompilerParams(vmem_limit_bytes=60 * 2**20),
        cost_estimate=pl.CostEstimate(
            flops=16 * tokens * width * wide, bytes_accessed=2**25, transcendentals=0
        ),
    )(returned, grad_top, hidden, entry, slope, w_up, w_down)


def tail_kernel(line, seqs, lag, *refs):
    refs = list(refs)

    def take(number):
        return [refs.pop(0) for _ in range(number)]

    scale, rest, factor_one, factor_two, embedded, noisy, w_in = take(7)
    far = take(9)
    parts = take(2)
    (head_part,) = take(1)
    outs = take(5)
    head_out, smalls, rows_all = take(3)
    near = take(9)
    grad_attn, grad_mixed, grad_joined, grad_first, grad_cond, in_weight = take(6)
    rows_own, small_wide, small_own = take(3)
    own, from_core, slots = take(2), take(5), take(5)
    head_own, head_core, head_section, last_total = take(4)
    far_sem, load_sem, core_send, core_recv, ring_send, ring_recv, credit = take(7)
    keep_sem, packet_send, packet_recv, wide_send, wide_recv, rows_send, rows_recv = take(7)
    head_sem, head_send, head_recv, cross_send, cross_recv = take(5)
    grad_middle, grad_entry, middle, x, joined, mixed, entry_attn, w_out, w_qkv = near
    inside = [w_qkv, w_out, in_weight]
    groups = ((0, 1), (2, 3, 4))
    chips = 2 * line
    width = x.shape[1]
    me_section = lax.axis_index("section")
    me_line = lax.axis_index("line")
    me_pair = lax.axis_index("pair")
    me_core = lax.axis_index("core")
    position = me_line + me_pair * (chips - 1 - 2 * me_line)
    section_peer = {"section": 1 - me_section}
    core_peer = {"core": 1 - me_core}
    ways = (1, -1)
    ring_peers = []
    for way in ways:
        peer_line, peer_pair = ring_place(lax.rem(position + way + chips, chips), line)
        ring_peers.append({"line": peer_line, "pair": peer_pair})
    greet([core_peer, section_peer] + ring_peers)

    shapes = [ref.shape[-2:] for ref in from_core]

    def block_of(turn, step):
        ahead = lax.rem(position - ways[turn] * (1 + step) + 2 * chips, chips)
        return ring_place(ahead, line)

    def portion(index, turn):
        high, wide = shapes[index]
        if high % 32 == 0:
            return turn * (high // 2), high // 2, 0, wide
        return 0, high, turn * (wide // 2), wide // 2

    def half_of(index, turn):
        first, rows, col, cols = portion(index, turn)
        return pl.ds(first, rows), pl.ds(col, cols)

    def inside_rows(index, place, pair, core, first, rows):
        base = ((place * 2 + pair) * 2 + core) * shapes[index][0] + first
        return pl.ds(pl.multiple_of(base, 16), rows)

    def source(index, turn, step, core):
        place, pair = block_of(turn, step)
        rows, cols = half_of(index, turn)
        if index < 2:
            return parts[index].at[place, pair, core, rows, cols]
        first, high = portion(index, turn)[:2]
        return inside[index - 2].at[inside_rows(index, place, pair, core, first, high), cols]

    def load(index, turn, step):
        return pltpu.make_async_copy(
            source(index, turn, step, me_core),
            own[index].at[(step % 2, *half_of(index, turn))],
            load_sem.at[index, turn, step],
        )

    def core_copy(index, turn, step):
        return remote(
            source(index, turn, step, 1 - me_core),
            from_core[index].at[(step % 3, *half_of(index, turn))],
            core_send.at[index, turn, step],
            core_recv.at[index, turn, step],
            core_peer,
        )

    def ring_copy(index, turn, step):
        half = half_of(index, turn)
        passed = from_core[index].at[(0, *half)] if step == 0 else slots[index].at[(step - 1, *half)]
        return remote(
            passed,
            slots[index].at[(step, *half)],
            ring_send.at[index, turn, step],
            ring_recv.at[index, turn, step],
            ring_peers[turn],
        )

    def to_core(group, step):
        if step >= 3:
            pl.semaphore_wait(credit.at[group], 1)
        for index in groups[group]:
            for turn in range(2):
                if index < 2:
                    load(index, turn, step).start()
                core_copy(index, turn, step).start()

    def stop(group, step, between):
        first, last = step == 0, step == chips - 1
        for index in groups[group]:
            for turn in range(2):
                start, rows, left, wide = portion(index, turn)
                tile = min(wide, 512)
                if index < 2:
                    load(index, turn, step).wait()
                core_copy(index, turn, step).wait_recv()
                if not first:
                    ring_copy(index, turn, step - 1).wait_recv()
                place, pair = block_of(turn, step)

                @pl.loop(0, rows // 16)
                def _(block):
                    row = pl.ds(pl.multiple_of(start + block * 16, 16), 16)
                    if index >= 2:
                        own_row = inside_rows(index, place, pair, me_core, start + block * 16, 16)
                    for col in range(left, left + wide, tile):
                        cols = pl.ds(col, tile)
                        if index < 2:
                            mine = own[index][step % 2, row, cols]
                        else:
                            mine = inside[index - 2][own_row, cols]
                        total = from_core[index][step % 3, row, cols].astype(f32)
                        total = total + mine.astype(f32)
                        if not first:
                            total = total + slots[index][step - 1, row, cols].astype(f32)
                        if last and index == 4:
                            last_total[row, cols] = total
                        elif last:
                            outs[index][row, cols] = total.astype(bf16)
                        elif first:
                            from_core[index][0, row, cols] = total.astype(bf16)
                        else:
                            slots[index][step - 1, row, cols] = total.astype(bf16)

                if not last:
                    ring_copy(index, turn, step).start()
                between()
        if step == 1:
            for index in groups[group]:
                for turn in range(2):
                    ring_copy(index, turn, 0).wait_send()
        if 1 <= step <= 4:
            amount = 2 if step == 1 else 1
            pl.semaphore_signal(
                credit.at[group], inc=amount, device_id=core_peer, device_id_type=MESH
            )

    hops = (line, line - 1)

    def packet_blocks(place, pair):
        return [smalls.at[place, pair, me_core], rows_all.at[place, pair, me_core]]

    def packet_hops(turn, hop, away):
        place, pair = ring_place(
            lax.rem(position - ways[turn] * (hop + away) + 2 * chips, chips), line
        )
        return [
            remote(
                block,
                block,
                packet_send.at[n, turn, hop],
                packet_recv.at[n, turn, hop],
                ring_peers[turn],
            )
            for n, block in enumerate(packet_blocks(place, pair))
        ]

    def pass_packets(hop):
        for turn in range(2):
            if 0 < hop <= hops[turn]:
                for copy in packet_hops(turn, hop - 1, 1):
                    copy.wait_recv()
            if hop < hops[turn]:
                for copy in packet_hops(turn, hop, 0):
                    copy.start()

    small_slot, rows_slot = packet_blocks(me_line, me_pair)
    keep_small = pltpu.make_async_copy(small_own, small_slot, keep_sem.at[0])
    keep_rows = pltpu.make_async_copy(rows_own, rows_slot, keep_sem.at[1])
    rows_over = remote(rows_own, rows_slot, rows_send, rows_recv, section_peer)
    across = [
        remote(block, block, wide_send.at[n], wide_recv.at[n], core_peer)
        for n, block in enumerate([smalls.at[:, :, me_core], rows_all.at[:, :, me_core]])
    ]
    def packets_ready():
        keep_small.wait()

        @pl.when(me_section == 0)
        def _():
            keep_rows.wait()

        @pl.when(me_section == 1)
        def _():
            rows_over.wait_recv()

    high = head_part.shape[0] // 4

    def shard(n):
        return head_part.at[pl.ds(n * high, high)]

    head_loads = [
        pltpu.make_async_copy(shard(2 * n), head_own.at[n], head_sem.at[n]) for n in range(2)
    ]
    head_copies = [
        remote(shard(2 * n + 1), head_core.at[n], head_send.at[n], head_recv.at[n], core_peer)
        for n in range(2)
    ]
    head_copies.append(
        remote(head_core.at[1], head_section, head_send.at[2], head_recv.at[2], section_peer)
    )

    def head_over_cores():
        for copy in head_loads:
            copy.wait()
        for copy in head_copies[:2]:
            copy.wait_recv()

        @pl.loop(0, high // 16)
        def _(block):
            rows = pl.ds(pl.multiple_of(block * 16, 16), 16)
            value = head_core[1, rows, :].astype(f32) + head_own[1, rows, :].astype(f32)
            head_core[1, rows, :] = value.astype(bf16)

        head_copies[2].start()

    def head_over_sections():
        head_copies[2].wait_recv()

        @pl.loop(0, high // 16)
        def _(block):
            rows = pl.ds(pl.multiple_of(block * 16, 16), 16)
            value = head_core[0, rows, :].astype(f32) + head_own[0, rows, :].astype(f32)
            value = value + head_section[rows, :].astype(f32)
            head_out[rows, :] = value.astype(bf16)

    far_copies = []
    for n, (where, target) in enumerate(zip(far, near)):
        where = where.at[0] if n >= 7 else where
        far_copies.append(pltpu.make_async_copy(where, target, far_sem.at[n]))

    def waits(*numbers):
        for n in numbers:
            far_copies[n].wait()

    def store_middle(rows, value):
        grad_middle[rows, :] = value
        grad_attn[rows, :] = value.astype(bf16)

    def store_first(rows, value):
        grad_first[rows, :] = value.astype(bf16)

    def second_norm(seq):
        if seq == 0:
            waits(0, 1, 2)
        norm_grads(middle, grad_entry, grad_middle, scale, grad_cond, 1, seq, store_middle)

    def mixed_grads(index):
        if index == 0:
            waits(7)
        part = pl.ds(index * 512, 512)
        grad_mixed[:, part] = nt(grad_attn[...], w_out[part, :]).astype(bf16)

    def heads_grads(pair):
        if pair == 0:
            waits(4)
        attention_grads(joined, grad_mixed, grad_joined, pair, seqs)

    def entry_grads(index):
        if index == 0:
            waits(8)
        part = pl.ds(index * 256, 256)
        grad_entry[:, part] = nt(grad_joined[...], w_qkv[part, :])

    def first_norm(seq):
        if seq == 0:
            waits(3)
        norm_grads(x, grad_entry, grad_middle, scale, grad_cond, 0, seq, store_first)

    def embedding_rows(_):
        grad_noisy = nt(grad_first[...], w_in[...])
        inner = jnp.mean(grad_noisy * embedded[...], -1, keepdims=True)
        value = factor_one[...] * grad_noisy - factor_two[...] * embedded[...] * inner
        rows_own[...] = value.astype(bf16)

        @pl.when(me_section == 0)
        def _():
            keep_rows.start()
            rows_over.start()

    def small_rows(_):
        each = small_wide.shape[1]
        for seq in range(seqs):
            for n in range(2 * width // each):
                row = pl.ds(seq * (2 * width // each) + n, 1)
                small_wide[row, :] = grad_cond[seq, :, pl.ds(n * each, each)]
        small_wide[pl.ds(seqs * 2 * width // each, rest.shape[0]), :] = rest[...]
        small_own[...] = small_wide[...].astype(bf16)
        keep_small.start()

    def input_weight(_):
        in_weight[...] = tn(noisy[...], grad_first[...]).astype(bf16)

    def qkv_weight(index):
        if index == 0:
            waits(6)
        part = pl.ds(index * 256, 256)
        w_qkv[part, :] = tn(entry_attn[:, part], grad_joined[...]).astype(bf16)

    def out_weight(index):
        if index == 0:
            waits(5)
        part = pl.ds(index * 512, 512)
        w_out[part, :] = tn(mixed[:, part], grad_attn[...]).astype(bf16)

    steps = []
    for step, number in (
        (second_norm, seqs),
        (mixed_grads, width // 512),
        (heads_grads, width // 128),
        (entry_grads, width // 256),
        (first_norm, seqs),
        (embedding_rows, 1),
        (small_rows, 1),
        (input_weight, 1),
        (qkv_weight, width // 256),
        (out_weight, width // 512),
    ):
        steps += [partial(step, n) for n in range(number)]
    at_once = -(-len(steps) // (4 * lag))

    def work():
        for _ in range(at_once):
            if steps:
                steps.pop(0)()

    def nothing():
        pass

    to_core(0, 0)
    to_core(0, 1)
    for copy in far_copies:
        copy.start()
    stop(0, 0, work)
    for turn in range(1, chips + lag):
        if turn + 1 < chips:
            to_core(0, turn + 1)
        if turn == 1:
            for copy in head_loads + head_copies[:2]:
                copy.start()
        if turn == lag:
            to_core(1, 0)
        if lag <= turn and turn - lag + 1 < chips:
            to_core(1, turn - lag + 1)
        if turn < chips:
            stop(0, turn, work if turn < lag else nothing)
        if turn >= lag:
            stop(1, turn - lag, nothing)
        hop = turn - lag - 2
        if hop == 0:
            packets_ready()
        if 0 <= hop <= line:
            pass_packets(hop)
        if hop == line:
            for copy in across:
                copy.start()
        if turn == 3:
            head_over_cores()
        if turn == chips + lag - 2:
            head_over_sections()
    each = outs[4].shape[0]
    give = remote(last_total.at[pl.ds(each, each)], outs[4], cross_send, cross_recv, section_peer)

    @pl.when(me_section == 0)
    def _():
        give.start()
        outs[4][...] = last_total[pl.ds(0, each), :]

    for copy in across:
        copy.wait()
    for copy in head_copies:
        copy.wait_send()
    for turn in range(2):
        for hop in range(hops[turn]):
            for copy in packet_hops(turn, hop, 0):
                copy.wait_send()
    for index in range(5):
        for turn in range(2):
            for step in range(chips):
                core_copy(index, turn, step).wait_send()
                if 0 < step < chips - 1:
                    ring_copy(index, turn, step).wait_send()

    @pl.when(me_section == 0)
    def _():
        rows_over.wait_send()
        give.wait_send()

    @pl.when(me_section == 1)
    def _():
        give.wait_recv()


def tail_pass(scale, rest, factors, embedded, noisy, w_in, far, parts, head_part, collective_id):
    grad_middle = far[0]
    tokens, width = grad_middle.shape
    seqs = scale.shape[0]
    line = parts[0].shape[0]
    chips = 2 * line
    count = 4 * line
    emb_width = noisy.shape[1]
    vmem = pl.BlockSpec(memory_space=pltpu.VMEM)
    anywhere = pl.BlockSpec(memory_space=pl.ANY)
    dma = pltpu.SemaphoreType.DMA
    shapes = [part.shape[-2:] for part in parts]
    shapes += [
        (width // count, 3 * width),
        (width // count, width),
        (emb_width // count, width),
    ]
    each = shapes[4][0] // 2
    high = head_part.shape[0] // 4
    small = (seqs * 2 * width // emb_width + rest.shape[0], emb_width)
    exact = ((tokens, width), f32)
    low = ((tokens, width), bf16)
    three = ((tokens, 3 * width), bf16)
    rows = (tokens, emb_width)
    results = [(shape, bf16) for shape in shapes[:4]]
    results += [((each, width), f32), ((high, width), bf16)]
    results += [((line, 2, 2) + small, bf16), ((line, 2, 2) + rows, bf16)]
    room = [exact, exact, exact, exact, three, low, low]
    room += [((width, width), bf16), ((width, 3 * width), bf16)]
    room += [low, low, three, low, ((seqs, 1, 2 * width), f32), ((emb_width, width), bf16)]
    room += [(rows, bf16), (small, f32), (small, bf16)]
    room += [((2,) + shape, bf16) for shape in shapes[:2]]
    room += [((3,) + shape, bf16) for shape in shapes]
    room += [((chips - 1,) + shape, bf16) for shape in shapes]
    room += [((2, high, width), bf16), ((2, high, width), bf16), ((high, width), bf16)]
    room += [(shapes[4], f32)]
    scratch = [pltpu.VMEM(*item) for item in room]
    scratch += [dma((9,)), dma((2, 2, chips)), dma((5, 2, chips)), dma((5, 2, chips))]
    scratch += [dma((5, 2, chips - 1)), dma((5, 2, chips - 1)), pltpu.SemaphoreType.REGULAR((2,))]
    scratch += [dma((2,)), dma((2, 2, line)), dma((2, 2, line)), dma((2,)), dma((2,)), dma, dma]
    scratch += [dma((2,)), dma((3,)), dma((3,)), dma, dma]
    return pl.pallas_call(
        partial(tail_kernel, line, seqs, line),
        out_shape=[jax.ShapeDtypeStruct(*item) for item in results],
        in_specs=[vmem] * 7 + [anywhere] * 12,
        out_specs=[vmem] * 6 + [anywhere] * 2,
        scratch_shapes=scratch,
        compiler_params=pltpu.CompilerParams(
            collective_id=collective_id, has_side_effects=True, vmem_limit_bytes=62 * 2**20
        ),
        cost_estimate=pl.CostEstimate(flops=0, bytes_accessed=2**29, transcendentals=0),
    )(scale, rest, *factors, embedded, noisy, w_in, *far, *parts, head_part)


def finish_kernel(line, head_rows, *refs):
    ids, rows, *lows = refs[:7]
    *exacts, grad_embed, total = refs[7:]
    me_section = lax.axis_index("section")
    me_line = lax.axis_index("line")
    me_pair = lax.axis_index("pair")
    me_core = lax.axis_index("core")
    high = total.shape[0]
    base = (((me_section * line + me_line) * 2 + me_pair) * 2 + me_core) * grad_embed.shape[0]
    tile = 768
    for index in range(rows.shape[0] // tile):
        part = pl.ds(index * tile, tile)
        entry = lax.broadcasted_iota(jnp.int32, (high, tile), 0) + base
        place = jnp.where(entry == ids[:, part], 1.0, 0.0).astype(bf16)
        product = nn(place, rows[part, :])
        total[...] = product if index == 0 else total[...] + product
    grad_embed[...] = total[pl.ds(0, grad_embed.shape[0]), :]
    for low, exact in zip(lows, exacts):
        whole = exact.shape[0] // 16
        left = exact.shape[0] % 16

        @pl.loop(0, whole)
        def _(block):
            part = pl.ds(pl.multiple_of(block * 16, 16), 16)
            exact[part, :] = low[part, :].astype(f32)

        if left:
            value = low[pl.ds(whole * 16, 16), :].astype(f32)
            exact[pl.ds(whole * 16, left), :] = value[:left]


def finish(ids, rows, lows, line, head_rows, out_rows):
    vmem = pl.BlockSpec(memory_space=pltpu.VMEM)
    shapes = [low.shape for low in lows[:-1]] + [(head_rows, lows[-1].shape[1])]
    shapes.append((out_rows, rows.shape[1]))
    return pl.pallas_call(
        partial(finish_kernel, line, head_rows),
        out_shape=[jax.ShapeDtypeStruct(shape, f32) for shape in shapes],
        in_specs=[vmem] * 7,
        out_specs=[vmem] * 6,
        scratch_shapes=[pltpu.VMEM((-(-out_rows // 16) * 16, rows.shape[1]), f32)],
        compiler_params=pltpu.CompilerParams(vmem_limit_bytes=60 * 2**20),
        cost_estimate=pl.CostEstimate(
            flops=2 * out_rows * rows.size, bytes_accessed=2**24, transcendentals=0
        ),
    )(ids, rows, *lows)


def norm_rows(values):
    centred = values - jnp.mean(values, -1, keepdims=True)
    factor = lax.rsqrt(jnp.mean(centred * centred, -1, keepdims=True) + epsilon)
    return (centred * factor, factor)


def norm_back(gradient, normed, factor):
    return factor * (
        gradient
        - jnp.mean(gradient, -1, keepdims=True)
        - normed * jnp.mean(gradient * normed, -1, keepdims=True)
    )


def time_features(noise_level):
    half_width = TFEAT // 2
    rates = jnp.exp(jnp.arange(half_width, dtype=f32) * (math.log(1000.0) / half_width))
    angles = (jnp.log(noise_level) / 4.0)[:, None] * rates[None, :]
    return jnp.concatenate([jnp.cos(angles), jnp.sin(angles)], -1)


def levels_of(bins, table):
    hits = bins[:, None] == jnp.arange(table.shape[0])[None, :]
    return jnp.sum(jnp.where(hits, table[None, :], 0.0), -1)


def over_dp(part):
    part = part.reshape((part.shape[0] // 4, 2, 2) + part.shape[1:])
    part = lax.psum_scatter(part, "core", scatter_dimension=2)
    part = lax.psum_scatter(part, "pair", scatter_dimension=1)
    return lax.psum_scatter(part, "line", scatter_dimension=0)


def by_owner(part):
    line = lax.axis_size("line")
    return part.astype(bf16).reshape((line, 2, 2, part.shape[0] // (line * 4)) + part.shape[1:])


def mm(spec, left, right):
    return jnp.einsum(spec, left, right, preferred_element_type=f32)


def layer_forward(stream, scale_attn, scale_mlp, weights):
    w_qkv, w_out, w_up, b_hidden, w_down = weights
    seq_count, length, model_width = stream.shape
    normed_attn, factor_attn = norm_rows(stream)
    attn_entry = (normed_attn * scale_attn).astype(bf16)
    joined = mm("nsd,de->nse", attn_entry, w_qkv).astype(bf16)
    qkv_parts = joined.reshape(seq_count, length, 3, HEADS, HEAD_DIM)
    query_rows = qkv_parts[:, :, 0]
    key_rows = qkv_parts[:, :, 1]
    value_rows = qkv_parts[:, :, 2]
    scores = mm("nqhe,nkhe->nhqk", query_rows, key_rows) / math.sqrt(HEAD_DIM)
    exp_scores = jnp.exp(scores - jnp.max(scores, -1, keepdims=True))
    attn_probs = exp_scores / jnp.sum(exp_scores, -1, keepdims=True)
    probs_low = attn_probs.astype(bf16)
    attn_mixed = mm("nhqk,nkhe->nqhe", probs_low, value_rows).astype(bf16)
    attn_mixed = attn_mixed.reshape(seq_count, length, model_width)
    middle = stream + mm("nsd,de->nse", attn_mixed, w_out)
    normed_mlp, factor_mlp = norm_rows(middle)
    mlp_entry = (normed_mlp * scale_mlp).astype(bf16)
    up_proj = mm("nsd,df->nsf", mlp_entry, w_up) + b_hidden
    below = 0.5 + 0.5 * lax.erf(up_proj * math.sqrt(0.5))
    hidden = (up_proj * below).astype(bf16)
    density = jnp.exp(-0.5 * up_proj * up_proj) * (1.0 / math.sqrt(2.0 * math.pi))
    slope = (below + up_proj * density).astype(bf16)
    block_out = middle + mm("nsf,fd->nsd", hidden, w_down)
    kept = (
        normed_attn,
        factor_attn,
        attn_entry,
        query_rows,
        key_rows,
        value_rows,
        attn_probs,
        probs_low,
        attn_mixed,
        normed_mlp,
        factor_mlp,
        mlp_entry,
        slope,
        hidden,
    )
    return (block_out, kept)


def layer_backward(grad_out, kept, scale_attn, scale_mlp, weights, whole):
    w_qkv, w_out, w_up, b_hidden, w_down = weights
    (
        normed_attn,
        factor_attn,
        attn_entry,
        query_rows,
        key_rows,
        value_rows,
        attn_probs,
        probs_low,
        attn_mixed,
        normed_mlp,
        factor_mlp,
        mlp_entry,
        slope,
        hidden,
    ) = kept
    seq_count, length, model_width = grad_out.shape
    grads = {}
    grad_branch = grad_out.astype(bf16)
    if whole:
        grads["down"] = by_owner(mm("nsf,nsd->fd", hidden, grad_branch))
    grad_hidden = mm("nsd,fd->nsf", grad_branch, w_down)
    grad_up_proj = (grad_hidden * slope.astype(f32)).astype(bf16)
    if whole:
        grads["bias"] = jnp.sum(grad_up_proj.astype(f32), (0, 1))
        grads["up"] = by_owner(mm("nsd,nsf->df", mlp_entry, grad_up_proj))
    grad_entry = mm("nsf,df->nsd", grad_up_proj, w_up)
    grad_middle = grad_out + norm_back(grad_entry * scale_mlp, normed_mlp, factor_mlp)
    grad_attn = grad_middle.astype(bf16)
    if whole:
        grads["out"] = by_owner(mm("nsd,nse->de", attn_mixed, grad_attn))
    grad_mixed = mm("nse,de->nsd", grad_attn, w_out)
    grad_mixed = grad_mixed.astype(bf16).reshape(seq_count, length, HEADS, HEAD_DIM)
    grad_probs = mm("nqhe,nkhe->nhqk", grad_mixed, value_rows)
    grad_values = mm("nhqk,nqhe->nkhe", probs_low, grad_mixed)
    grad_scores = (
        attn_probs * (grad_probs - jnp.sum(grad_probs * attn_probs, -1, keepdims=True))
    ).astype(bf16)
    grad_query = mm("nhqk,nkhe->nqhe", grad_scores, key_rows) / math.sqrt(HEAD_DIM)
    grad_keys = mm("nhqk,nqhe->nkhe", grad_scores, query_rows) / math.sqrt(HEAD_DIM)
    grad_joined = jnp.stack([grad_query, grad_keys, grad_values], 2).astype(bf16)
    grad_joined = grad_joined.reshape(seq_count, length, 3 * model_width)
    if whole:
        grads["qkv"] = by_owner(mm("nsd,nse->de", attn_entry, grad_joined))
    grad_attn_entry = mm("nse,de->nsd", grad_joined, w_qkv)
    grad_stream = grad_middle + norm_back(grad_attn_entry * scale_attn, normed_attn, factor_attn)
    if whole:
        grads["cond"] = jnp.concatenate(
            [jnp.sum(grad_attn_entry * normed_attn, 1), jnp.sum(grad_entry * normed_mlp, 1)], -1
        )
    return (grad_stream, grads)


def local(
    token_ids,
    target_ids,
    time_bins,
    sigma_table,
    noise,
    embed,
    w_in,
    w_time,
    norm_gain,
    w_qkv,
    w_out,
    w_up,
    b_hidden,
    w_down,
    out_gain,
    head,
):
    section = lax.axis_index("section")
    line_at = lax.axis_index("line")
    pair_at = lax.axis_index("pair")
    core = lax.axis_index("core")
    sections = lax.axis_size("section")
    line = lax.axis_size("line")
    chip = line_at * 2 + pair_at
    chips = line * 2
    cores = 2
    dp_count = chips * cores
    dp_index = chip * cores + core
    is_first = section == 0
    seqs, length = token_ids.shape
    tokens = seqs * length
    half = tokens // sections
    model_width = w_out.shape[-1]
    emb_rows, emb_width = embed.shape
    head_rows = head.shape[0]
    straight = line <= 4 and half % 16 == 0 and model_width // dp_count % 16 == 0

    if straight:
        lanes = -(-half // 128) * 128
        blocks = [part.reshape(2, half) for part in (token_ids, target_ids)]
        blocks.append(jnp.pad(time_bins[None, :], ((0, 0), (0, half - seqs))))
        own_ids = jnp.pad(jnp.concatenate(blocks, 0), ((0, 3), (0, lanes - half)))
        head_own = jnp.pad(head, ((0, -head_rows % 512), (0, 0)))
        all_ids, embedded, head_early, head_core = start_pass(
            own_ids, embed, head_own, half, line, 0
        )
        all_ids = all_ids.reshape(dp_count, 8, lanes)
        all_tokens = all_ids[:, 0:2, :half].reshape(dp_count, tokens)
        all_targets = all_ids[:, 2:4, :half].reshape(dp_count, tokens)
        all_bins = all_ids[:, 4, :seqs].reshape(-1)
        embedded = embedded.swapaxes(1, 2)
    else:
        own_ids = jnp.concatenate([token_ids.reshape(-1), target_ids.reshape(-1), time_bins])
        all_ids = lax.all_gather(own_ids, DP)
        all_tokens = all_ids[:, :tokens]
        all_targets = all_ids[:, tokens : 2 * tokens]
        all_bins = all_ids[:, 2 * tokens :].reshape(-1)
        own_rows = dp_index * emb_rows + jnp.arange(emb_rows)
        half_tokens = lax.dynamic_slice_in_dim(all_tokens, section * half, half, 1)
        picked = (half_tokens.reshape(-1)[:, None] == own_rows[None, :]).astype(bf16)
        found = jnp.dot(picked, embed, preferred_element_type=f32).astype(bf16)
        embedded = lax.all_gather(over_dp(found.reshape(dp_count, half, emb_width)), "section")
    embedded = embedded.astype(f32).reshape(seqs, length, emb_width)

    swapped = [(0, 1), (1, 0)]
    if not straight:
        head_group = lax.all_gather(lax.all_gather(head, "core"), "section")
        head_group = head_group.reshape(-1, model_width)
        vocab_base = (
            (jnp.arange(sections)[:, None] * chips + chip) * cores + jnp.arange(cores)[None, :]
        ) * head_rows
        columns = (vocab_base[:, :, None] + jnp.arange(head_rows)[None, None, :]).reshape(-1)

    noise_level = levels_of(time_bins, sigma_table)
    unit_factor = lax.rsqrt(jnp.mean(embedded * embedded, -1, keepdims=True) + epsilon)
    level_col = noise_level[:, None, None]
    noise_scale = lax.rsqrt(level_col * level_col + 1.0)
    noisy_rows = ((embedded * unit_factor + level_col * noise) * noise_scale).astype(bf16)
    time_feats = time_features(noise_level)
    conditioned = jnp.dot(time_feats, w_time[0].astype(f32), precision=highest) + norm_gain[0]
    scale_attn = conditioned[:, None, :model_width]
    scale_mlp = conditioned[:, None, model_width:]
    scale = conditioned[:, None, :]
    weights = (w_qkv[0], w_out[0], w_up[0], b_hidden[0], w_down[0])
    stacked = (w_qkv, w_out, w_up, b_hidden, w_down)
    stream0 = mm("nse,ed->nsd", noisy_rows, w_in)
    flat = (tokens, model_width)
    if straight:
        block_out, final_rows, *kept, head_late, head_fourth = forward_pass(
            stream0.reshape(flat), scale, stacked, out_gain[None, :], head_own, head_early, 1
        )
        heads = [head_own, head_core, head_early, head_late, head_fourth]
    else:
        first_out = layer_forward(stream0, scale_attn, scale_mlp, weights)[0].astype(bf16)
        arrived = lax.ppermute(first_out, "section", swapped)
        stream = jnp.where(is_first, stream0, arrived.astype(f32))
        block_out, kept = layer_forward(stream, scale_attn, scale_mlp, weights)
        final_normed, final_factor = norm_rows(block_out.astype(bf16).astype(f32))
        final_rows = (final_normed * out_gain).astype(bf16).reshape(flat)

    targets_group = lax.dynamic_slice_in_dim(
        all_targets.reshape(chips, cores, tokens), core, 1, 1
    )[:, 0]
    targets_group = lax.dynamic_slice_in_dim(targets_group, section * half, half, 1)
    if straight:
        grad_final, grad_head, lse, picks = head_pass(
            final_rows, targets_group.reshape(line, 1, tokens), heads, line, head_rows, length, 3
        )
        ce_part = jnp.sum(lse) / chips - jnp.sum(picks)
    else:
        targets_group = targets_group.reshape(-1)
        handed = lax.ppermute(final_rows[:half], "section", [(1, 0), (0, 1)])
        own_final = jnp.where(is_first, handed, final_rows[half:])
        group_final = lax.all_gather(own_final, ("line", "pair"), tiled=True)
        logits = mm("td,vd->tv", group_final, head_group)
        local_top = jnp.max(logits, -1)
        local_total = jnp.sum(jnp.exp(logits - local_top[:, None]), -1)
        mark = columns[None, :] == targets_group[:, None]
        local_pick = jnp.sum(jnp.where(mark, logits, 0.0))
        stats = lax.all_gather(jnp.stack([local_top, local_total]), ("line", "pair"))
        all_top = jnp.max(stats[:, 0], 0)
        all_total = jnp.sum(stats[:, 1] * jnp.exp(stats[:, 0] - all_top), 0)
        log_total = all_top + jnp.log(all_total)
        soft_rows = jnp.exp(logits - log_total[:, None])
        logit_grads = ((soft_rows - jnp.where(mark, 1.0, 0.0)) / length).astype(bf16)
        grad_final = jnp.dot(logit_grads, head_group, preferred_element_type=f32).astype(bf16)
        grad_final = lax.psum_scatter(grad_final, ("line", "pair"), scatter_dimension=0, tiled=True)
        handed = lax.ppermute(grad_final, "section", swapped)
        grad_final = jnp.concatenate([handed, grad_final], 0)
        grad_head = mm("tv,td->vd", logit_grads, group_final).astype(bf16)
        grad_head = grad_head.reshape(sections, cores, head_rows, model_width)
        grad_head = lax.psum_scatter(grad_head, "core", scatter_dimension=1)
        grad_head = lax.psum_scatter(grad_head, "section", scatter_dimension=0).astype(f32)

        ce_part = jnp.sum(log_total) / chips - local_pick
    if straight:
        grad_second, grad_top, out_part = backward_pass(
            grad_final, block_out, out_gain[None, :], scale, kept, stacked
        )
        returned = lax.ppermute(grad_second, "section", swapped)
        out_part = out_part.reshape(-1)
        x, joined, mixed, middle, entry_attn, entry_mlp, slope, hidden = kept
        grad_middle, grad_entry, grad_bias, down_part, up_part = backward_begin(
            returned, grad_top, seqs, hidden, entry_mlp, slope, w_up, w_down
        )
        parts = [by_owner(down_part), by_owner(up_part)]
        grad_bias = grad_bias.reshape(-1)
    else:
        grad_final = grad_final.astype(f32).reshape(stream0.shape)
        out_part = jnp.sum(grad_final * final_normed, (0, 1))
        grad_top = norm_back(grad_final * out_gain, final_normed, final_factor)
        grad_second = layer_backward(grad_top, kept, scale_attn, scale_mlp, weights, False)[0]
        returned = lax.ppermute(grad_second.astype(bf16), "section", swapped)
        grad_cot = jnp.where(is_first, returned.astype(f32), grad_top)
        grad_stream, grads = layer_backward(grad_cot, kept, scale_attn, scale_mlp, weights, True)
        grad_first = grad_stream.astype(bf16)
    out_part = jnp.where(is_first, 0.0, out_part)

    ce_high = ce_part.astype(bf16).astype(f32)
    ce_mid = (ce_part - ce_high).astype(bf16).astype(f32)
    ce_low = ce_part - ce_high - ce_mid
    shared = jnp.concatenate([out_part, jnp.stack([ce_high, ce_mid, ce_low])])
    shared_rows = -(-shared.shape[0] // emb_width)
    shared = jnp.pad(shared, (0, shared_rows * emb_width - shared.shape[0]))
    shared = shared.reshape(-1, emb_width).astype(bf16)
    both = [shared, lax.ppermute(shared, "section", swapped)]

    cubed = unit_factor * unit_factor * unit_factor
    cond_rows = seqs * 2 * model_width // emb_width
    bias_rows = b_hidden.shape[1] // emb_width
    if straight:
        rest = jnp.concatenate([grad_bias.reshape(-1, emb_width)] + both, 0).astype(f32)
        rest = jnp.pad(rest, ((0, -(cond_rows + rest.shape[0]) % 16), (0, 0)))
        factors = [
            (value * noise_scale).reshape(tokens, 1) for value in (unit_factor, cubed)
        ]
        owned = noisy_rows.reshape(tokens, sections, dp_count, -1)
        owned = owned.swapaxes(1, 2).reshape(tokens, emb_width)
        far = [grad_middle, grad_entry, middle, x, joined, mixed, entry_attn, w_out, w_qkv]
        grad_down, grad_up, grad_qkv, grad_wout, grad_w_in, grad_head, smalls, rows_all = tail_pass(
            scale,
            rest,
            factors,
            embedded.reshape(tokens, emb_width),
            owned,
            w_in,
            far,
            parts,
            grad_head,
            2,
        )
        ids = all_tokens.reshape(1, -1)
        grad_down, grad_up, grad_qkv, grad_wout, grad_head, grad_embed = finish(
            ids,
            rows_all.reshape(-1, emb_width),
            [grad_down, grad_up, grad_qkv, grad_wout, grad_head],
            line,
            head_rows,
            emb_rows // sections,
        )
    else:
        in_part = mm("nse,nsd->ed", noisy_rows, grad_first).astype(bf16)
        in_part = in_part.reshape(sections, dp_count, -1, model_width).swapaxes(0, 1)
        in_sum = over_dp(in_part).astype(f32)
        in_handed = lax.ppermute(in_sum[1], "section", swapped)
        grad_w_in = jnp.where(is_first, in_sum[0], in_handed)
        grad_noisy = mm("nsd,ed->nse", grad_first, w_in)
        grad_unit = grad_noisy * noise_scale
        grad_embedded = unit_factor * grad_unit - cubed * embedded * jnp.mean(
            grad_unit * embedded, -1, keepdims=True
        )
        grad_flat = grad_embedded.reshape(tokens, emb_width).astype(bf16)
        handed = lax.ppermute(grad_flat, "section", swapped)
        rows_all = lax.all_gather(jnp.where(is_first, grad_flat, handed), DP)
        small = [grads["cond"].reshape(-1, emb_width), grads["bias"].reshape(-1, emb_width)]
        smalls = lax.all_gather(
            jnp.concatenate([value.astype(bf16) for value in small] + both, 0), DP
        )
        grad_down, grad_up, grad_qkv, grad_wout = [
            over_dp(part.reshape((dp_count,) + part.shape[3:])).astype(f32)
            for part in (grads["down"], grads["up"], grads["qkv"], grads["out"])
        ]
        grad_all = rows_all.reshape(-1, emb_width)
        out_rows = emb_rows // sections
        target_rows = (section * dp_count + dp_index) * out_rows + jnp.arange(out_rows)
        place = (target_rows[:, None] == all_tokens.reshape(-1)[None, :]).astype(bf16)
        grad_embed = jnp.dot(place, grad_all, preferred_element_type=f32)

    smalls = smalls.reshape(dp_count, -1, emb_width).astype(f32)
    cond_all = smalls[:, :cond_rows].reshape(dp_count * seqs, 2 * model_width)
    bias_all = smalls[:, cond_rows : cond_rows + bias_rows].reshape(dp_count, -1)
    hidden_rows = bias_all.shape[1] // dp_count
    grad_bias = jnp.sum(
        lax.dynamic_slice_in_dim(bias_all, dp_index * hidden_rows, hidden_rows, 1), 0
    )
    norm_cols = 2 * model_width // dp_count
    grad_gain = jnp.sum(lax.dynamic_slice_in_dim(cond_all, dp_index * norm_cols, norm_cols, 1), 0)
    feats_all = time_features(levels_of(all_bins, sigma_table))
    feat_rows = TFEAT // dp_count
    feats_own = lax.dynamic_slice_in_dim(feats_all, dp_index * feat_rows, feat_rows, 1)
    grad_time = jnp.dot(feats_own.T, cond_all, precision=highest)
    shared_first = cond_rows + bias_rows
    both = smalls[:, shared_first : shared_first + 2 * shared_rows]
    both = jnp.sum(both.reshape(dp_count, 2, -1), (0, 1))
    loss = jnp.sum(both[model_width : model_width + 3]) / (tokens * dp_count)
    gain_rows = model_width // dp_count
    grad_out_gain = lax.dynamic_slice_in_dim(both, dp_index * gain_rows, gain_rows)
    return (
        loss,
        grad_embed,
        grad_w_in,
        grad_time[None],
        grad_gain[None],
        grad_qkv[None],
        grad_wout[None],
        grad_up[None],
        grad_bias[None],
        grad_down[None],
        grad_out_gain,
        grad_head,
    )


def solution(mesh):
    sections, dp_count = mesh.shape["section"], mesh.shape["dp"]
    fine = Mesh(mesh.devices.reshape(sections, dp_count // 4, 2, 2), ("section",) + DP)
    everywhere = ("section",) + DP
    in_specs = (
        P(DP, None),
        P(DP, None),
        P(DP),
        P(),
        P(DP, None, None),
        P(DP, None),
        P(),
        P("section", None, None),
        P("section", None),
        P("section", None, None),
        P("section", None, None),
        P("section", None, None),
        P("section", None),
        P("section", None, None),
        P(),
        P(everywhere, None),
    )
    out_specs = (
        P(),
        P(everywhere, None),
        P(everywhere, None),
        P("section", DP, None),
        P("section", DP),
        P("section", DP, None),
        P("section", DP, None),
        P("section", DP, None),
        P("section", DP),
        P("section", DP, None),
        P(DP),
        P(everywhere, None),
    )
    return jax.shard_map(local, mesh=fine, in_specs=in_specs, out_specs=out_specs, check_vma=False)
```

profile of v0, /device:TPU:0, one launch (start us, length us, event | category | flops | bytes accessed | tf_op | source)
XLA Modules:
  0.0 485.6 jit_solution(13508345411834299051)
XLA Ops:
  0.7 0.9 reshape.189
  1.6 0.8 reshape.188
  3.0 1.7 pad.23.refs_2_.refs_8_
  4.8 40.1 %shard_map.247 = (s32[4,2,2,8,256]{4,3,2,1,0:T(8,128)S(1)}, bf16[2,256,192]{2,1,0:T(8,128)(2,1)S(1)}, bf16[640,1024]{1,0:T(8,128)(2,1)S(1)}, bf16[1024,1024]{1,0:T(8,128)(2,1)S(1)}) custom-call(s32[8,256]{1,0:T(8,128)S(1)} %pad.22.refs_0_, bf16[2000,256]{1,0:T(8,128)(2,1)S(1)} %copy-done.3, bf16[1024,1024]{1,0:T(8,128)(2,1)S(1)} %pad.23.refs_2_.refs_8_), custom_call_target="tpu_custom_call" | custom-call | bytes 134217728 | tf_op jit(solution)/shard_map/pallas_call | solution.py:187
  44.9 1.4 copy-done.4
  46.3 1.1 copy-done.5
  50.4 1.5 fusion.1
  51.9 47.3 %shard_map.248 = (bf16[384,1024]{1,0:T(8,128)(2,1)}, bf16[384,1024]{1,0:T(8,128)(2,1)}, f32[384,1024]{1,0:T(8,128)}, bf16[384,3072]{1,0:T(8,128)(2,1)}, bf16[384...) custom-call(f32[384,1024]{1,0:T(8,128)} %bitcast.57, ...), custom_call_target="tpu_custom_call" | custom-call | flops 38654705664 | bytes 33554432 | tf_op jit(solution)/shard_map/pallas_call | solution.py:870
  99.3 129.1 %shard_map.249 = (bf16[384,1024]{1,0:T(8,128)(2,1)}, bf16[4096,1024]{1,0:T(8,128)(2,1)}, f32[4,1,384]{2,1,0:T(1,128)}, f32[4,1,384]{2,1,0:T(1,128)}) custom-call(bf16[384,1024]{1,0:T(8,128)(2,1)} %get-tuple-element.56.refs_0_, s32[4,1,384]{2,1,0:T(1,128)} %reshape.209.refs_1_, bf16[1024,1024]{1,0:T(8,128)(2,1)} %copy-done.2, bf16[1024,1024]{1,0:T(8,128)(2,1)} %copy-done.4, ...), custom_call_target="tpu_custom_call" | custom-call | flops 38654705664 | bytes 268435456 | tf_op jit(solution)/shard_map/pallas_call | solution.py:620
  228.4 1.3 reduce_sum.90
  229.7 1.3 reduce_sum.91
  232.3 31.4 %shard_map.250 = (bf16[384,1024]{1,0:T(8,128)(2,1)}, f32[384,1024]{1,0:T(8,128)}, f32[1,1024]{1,0:T(1,128)}) custom-call(f32[3,1,2048]{2,1,0:T(1,128)} %broadcast_in_dim.72.refs_1_.refs_0_, bf16[384,1024]{1,0:T(8,128)(2,1)} %get-tuple-element.61.refs_1_, bf16[384,1024]{1,0:T(8,128)(2,1)} %get-tuple-element.62.refs_2_, f32[1,1024]{1,0:T(1,128)} %bitcast.70, ...), custom_call_target="tpu_custom_call" | custom-call | flops 19327352832 | bytes 33554432 | tf_op jit(solution)/shard_map/pallas_call | solution.py:1082
  264.0 2.0 collective-permute-start
  268.0 0.8 copy.66.refs_2_
  269.0 0.8 copy.67.refs_5_
  270.5 5.7 %collective-permute-done.refs_0_ = bf16[384,1024]{1,0:T(8,128)(2,1)S(1)} collective-permute-done((bf16[384,1024]{1,0:T(8,128)(2,1)}, bf16[384,1024]{1,0:T(8,128)(2,1)S(1)}, u32[]{:S(2)}, u32[]{:S(2)}) %collective-permute-start) | collective-permute-done | bytes 786464 | tf_op jit(solution)/shard_map/ppermute | solution.py:1912
  276.3 0.9 copy-done.12
  277.2 25.9 %shard_map.251 = (f32[384,1024]{1,0:T(8,128)}, f32[384,1024]{1,0:T(8,128)}, f32[1,4096]{1,0:T(1,128)}, bf16[4096,1024]{1,0:T(8,128)(2,1)}, bf16[1024,4096]{1,0:T(8,128)(2,1)}) custom-call(bf16[384,1024]{1,0:T(8,128)(2,1)} %copy-done.12, f32[384,1024]{1,0:T(8,128)} %get-tuple-element.68.refs_1_, bf16[384,4096]{1,0:T(8,128)(2,1)} %get-tuple-element.69.refs_2_, ...), custom_call_target="tpu_custom_call" | custom-call | flops 25769803776 | bytes 33554432 | tf_op jit(solution)/shard_map/pallas_call | solution.py:1105
  303.6 1.4 reduce.10
  305.6 160.6 %shard_map.252 = (bf16[256,1024]{1,0:T(8,128)(2,1)}, bf16[64,4096]{1,0:T(8,128)(2,1)}, bf16[64,3072]{1,0:T(8,128)(2,1)}, bf16[64,1024]{1,0:T(8,128)(2,1)}, f32[8...) custom-call(f32[3,1,2048]{2,1,0:T(1,128)} %broadcast_in_dim.72.refs_, ...), custom_call_target="tpu_custom_call" | custom-call | bytes 536870912 | tf_op jit(solution)/shard_map/pallas_call | solution.py:1570
  466.3 1.1 bitcast_convert_fusion
  468.2 0.9 slice.36
  471.8 1.0 convolution_bitcast_fusion
  472.8 10.6 %shard_map.253 = (f32[256,1024]{1,0:T(8,128)}, f32[64,4096]{1,0:T(8,128)}, f32[64,3072]{1,0:T(8,128)}, f32[64,1024]{1,0:T(8,128)}, f32[1000,1024]{1,0:T(8,128)}, /*index=5*/f32[1000,256]{1,0:T(8,128)}) custom-call(s32[1,6144]{1,0:T(1,128)} %reshape_reshape.15.refs_0_, bf16[6144,256]{1,0:T(8,128)(2,1)} %bitcast.68, ...), custom_call_target="tpu_custom_call" | custom-call | flops 3145728000 | bytes 16777216 | tf_op jit(solution)/shard_map/pallas_call | solution.py:1618
  (83 shorter events, 11.1 us)
Async XLA Ops:
  0.6 47.2 %copy-start = (bf16[1,256,2048]{2,1,0:T(8,128)(2,1)S(1)}, bf16[1,256,2048]{2,1,0:T(8,128)(2,1)}, u32[]{:S(2)}) copy-start(bf16[1,256,2048]{2,1,0:T(8,128)(2,1)} %param.23) | copy-start | bytes 3145732
  0.7 4.1 copy-start.3
  4.8 43.1 %copy-start.2 = (bf16[1024,1024]{1,0:T(8,128)(2,1)}, bf16[1024,1024]{1,0:T(8,128)(2,1)S(1)}, u32[]{:S(2)}) copy-start(bf16[1024,1024]{1,0:T(8,128)(2,1)S(1)} %pad.23.refs_2_.refs_8_) | copy-start | bytes 6291460
  4.8 42.7 %copy-start.11 = (s32[3]{0:T(128)S(1)}, s32[3]{0:T(128)}, u32[]{:S(2)}) copy-start(s32[3]{0:T(128)} %param.18) | copy-start | bytes 40
  4.8 42.7 %copy-start.13 = (f32[128]{0:T(128)S(1)}, f32[128]{0:T(128)}, u32[]{:S(2)}) copy-start(f32[128]{0:T(128)} %param.19) | copy-start | bytes 1540
  4.8 43.1 %copy-start.10 = (f32[1,2048]{1,0:T(1,128)S(1)}, f32[1,2048]{1,0:T(1,128)}, u32[]{:S(2)}) copy-start(f32[1,2048]{1,0:T(1,128)} %param.24) | copy-start | bytes 24580
  44.9 1.4 copy-start.4
  46.3 1.1 copy-start.5
  47.4 2.9 copy-start.8
  47.4 3.0 copy-start.7
  49.2 50.0 %copy-start.6 = (f32[2,192,256]{2,1,0:T(8,128)}, f32[2,192,256]{2,1,0:T(8,128)S(1)}, u32[]{:S(2)}) copy-start(f32[2,192,256]{2,1,0:T(8,128)S(1)} %copy.58) | copy-start | bytes 1179652
  263.9 6.7 %collective-permute-start.1 = (bf16[5,256]{1,0:T(8,128)(2,1)S(1)}, bf16[5,256]{1,0:T(8,128)(2,1)S(1)}, u32[]{:S(2)}, u32[]{:S(2)}) collective-permute-start(bf16[5,256]{1,0:T(8,128)(2,1)S(1)} %convert_element_type.48), channel_id=1, source_target_pairs={{0,16},{16,0},{1,17},{17,1},{2,18},{18,2},{3,19},{19,3},{4,20},{20... | collective-permute-start | bytes 7688 | tf_op jit(solution)/shard_map/ppermute | solution.py:1938
  264.0 12.3 %collective-permute-start = (bf16[384,1024]{1,0:T(8,128)(2,1)}, bf16[384,1024]{1,0:T(8,128)(2,1)S(1)}, u32[]{:S(2)}, u32[]{:S(2)}) collective-permute-start(bf16[384,1024]{1,0:T(8,128)(2,1)} %get-tuple-element.67), channel_id=1, source_target_pairs={{0,16},{16,0},{1,17},{17,1},{2,18},{18,2},{3,19},{19,3},{4,20},{20... | collective-permute-start | bytes 2359304 | tf_op jit(solution)/shard_map/ppermute | solution.py:1912
  276.3 0.9 copy-start.12
  472.8 10.6 %copy-start.9 = (f32[8,1024]{1,0:T(8,128)S(1)}, f32[8,1024]{1,0:T(8,128)}, u32[]{:S(2)}) copy-start(f32[8,1024]{1,0:T(8,128)} %get-tuple-element.121) | copy-start | bytes 98308
  472.8 11.2 %copy-start.1 = (bf16[1,256,2048]{2,1,0:T(8,128)(2,1)S(1)}, bf16[1,256,2048]{2,1,0:T(8,128)(2,1)}, u32[]{:S(2)}) copy-start(bf16[1,256,2048]{2,1,0:T(8,128)(2,1)} %param.23) | copy-start | bytes 3145732
where the time goes:
time: 493 us; the launch traced here: 486 us
  Pallas kernels  445 us (90%)
  local copies, waits for them, and re-layouts  15.2 us (3%)
  other arithmetic  9.89 us (2%)
  waiting for transfers between devices  5.74 us (1%)
    pallas_call x1, Pallas kernels, tail_pass(): pl.pallas_call(partial(tail_kernel, line, seqs, line), out_shape=[jax.Sha...  161 us
    pallas_call x1, Pallas kernels, head_pass(): pl.pallas_call(partial(head_kernel, line, head_rows, length), out_shape=[...  129 us
    pallas_call x1, Pallas kernels, forward_pass(): pl.pallas_call(partial(forward_kernel, seqs), out_shape=[jax.ShapeDtypeSt...  47.3 us
    pallas_call x1, Pallas kernels, start_pass(): pl.pallas_call(partial(start_kernel, line), out_shape=[jax.ShapeDtypeStru...  40.1 us
    pallas_call x1, Pallas kernels, backward_pass(): pl.pallas_call(partial(backward_kernel, False, scale.shape[0]), out_shape...  31.4 us
    pallas_call x1, Pallas kernels, backward_begin(): pl.pallas_call(partial(backward_kernel, True, seqs), out_shape=[jax.Shape...  25.9 us
    pallas_call x1, Pallas kernels, finish(): pl.pallas_call(partial(finish_kernel, line, head_rows), out_shape=[jax.Sh...  10.6 us
  transfers between devices with their start and end apart: 2, of which 1 were waited for; matrix products, arithmetic and copies ran while one was open for 1% of the time, Pallas kernels for 0%

commit v1 on v0

--- a/solution.py
+++ b/solution.py
@@ -181,7 +181,7 @@
     rows, width = embed.shape
     high = -(-rows // 256) * 256
     vmem = pl.BlockSpec(memory_space=pltpu.VMEM)
-    anywhere = pl.BlockSpec(memory_space=pl.ANY)
+    anywhere = pl.BlockSpec(memory_space=pltpu.HBM)
     dma = pltpu.SemaphoreType.DMA
     block = (width, half)
     return pl.pallas_call(
@@ -216,7 +216,7 @@
             dma((2,)),
         ],
         compiler_params=pltpu.CompilerParams(
-            collective_id=collective_id, has_side_effects=True, vmem_limit_bytes=40 * 2**20
+            collective_id=collective_id, has_side_effects=True, vmem_limit_bytes=60 * 2**20
         ),
         cost_estimate=pl.CostEstimate(flops=0, bytes_accessed=2**27, transcendentals=0),
     )(ids, embed, head)
@@ -614,7 +614,7 @@
     half = tokens // 2
     padded = heads[0].shape[0]
     vmem = pl.BlockSpec(memory_space=pltpu.VMEM)
-    anywhere = pl.BlockSpec(memory_space=pl.ANY)
+    anywhere = pl.BlockSpec(memory_space=pltpu.HBM)
     dma = pltpu.SemaphoreType.DMA
     peers = 2 * line - 1
     return pl.pallas_call(
@@ -857,6 +857,8 @@
     vmem = pl.BlockSpec(memory_space=pltpu.VMEM)
     anywhere = pl.BlockSpec(memory_space=pl.ANY)
 
+    far = pl.BlockSpec(memory_space=pltpu.HBM)
+
     def low(columns):
         return (tokens, columns), bf16
 
@@ -870,8 +872,8 @@
     return pl.pallas_call(
         partial(forward_kernel, seqs),
         out_shape=[jax.ShapeDtypeStruct(*item) for item in results],
-        in_specs=[vmem] * 4 + [anywhere] * 6,
-        out_specs=[vmem] * (len(results) - 2) + [anywhere] * 2,
+        in_specs=[vmem] * 4 + [anywhere] * 4 + [far] * 2,
+        out_specs=[vmem] * (len(results) - 2) + [far] * 2,
         scratch_shapes=scratch + [dma((4,)), dma((seqs,)), dma((seqs,)), dma((2,)), dma((2,))],
         compiler_params=pltpu.CompilerParams(
             collective_id=collective_id, has_side_effects=True, vmem_limit_bytes=60 * 2**20
@@ -1124,7 +1126,7 @@
     def take(number):
         return [refs.pop(0) for _ in range(number)]
 
-    scale, rest, factor_one, factor_two, embedded, noisy, w_in = take(7)
+    scale, bias_grad, rest, factor_one, factor_two, embedded, noisy, w_in = take(8)
     far = take(9)
     parts = take(2)
     (head_part,) = take(1)
@@ -1419,7 +1421,11 @@
             for n in range(2 * width // each):
                 row = pl.ds(seq * (2 * width // each) + n, 1)
                 small_wide[row, :] = grad_cond[seq, :, pl.ds(n * each, each)]
-        small_wide[pl.ds(seqs * 2 * width // each, rest.shape[0]), :] = rest[...]
+        first = seqs * 2 * width // each
+        for n in range(bias_grad.shape[1] // each):
+            small_wide[pl.ds(first + n, 1), :] = bias_grad[:, pl.ds(n * each, each)]
+        first += bias_grad.shape[1] // each
+        small_wide[pl.ds(first, rest.shape[0]), :] = rest[...]
         small_own[...] = small_wide[...].astype(bf16)
         keep_small.start()
 
@@ -1463,9 +1469,11 @@
         pass
 
     to_core(0, 0)
+    for copy in far_copies[:3]:
+        copy.start()
     to_core(0, 1)
-    for copy in far_copies:
-        copy.start()
+    for n in (7, 4, 8, 3, 6, 5):
+        far_copies[n].start()
     stop(0, 0, work)
     for turn in range(1, chips + lag):
         if turn + 1 < chips:
@@ -1526,7 +1534,9 @@
         give.wait_recv()
 
 
-def tail_pass(scale, rest, factors, embedded, noisy, w_in, far, parts, head_part, collective_id):
+def tail_pass(
+    scale, bias_grad, rest, factors, embedded, noisy, w_in, far, parts, head_part, collective_id
+):
     grad_middle = far[0]
     tokens, width = grad_middle.shape
     seqs = scale.shape[0]
@@ -1545,7 +1555,7 @@
     ]
     each = shapes[4][0] // 2
     high = head_part.shape[0] // 4
-    small = (seqs * 2 * width // emb_width + rest.shape[0], emb_width)
+    small = ((seqs * 2 * width + bias_grad.shape[1]) // emb_width + rest.shape[0], emb_width)
     exact = ((tokens, width), f32)
     low = ((tokens, width), bf16)
     three = ((tokens, 3 * width), bf16)
@@ -1570,14 +1580,14 @@
     return pl.pallas_call(
         partial(tail_kernel, line, seqs, line),
         out_shape=[jax.ShapeDtypeStruct(*item) for item in results],
-        in_specs=[vmem] * 7 + [anywhere] * 12,
+        in_specs=[vmem] * 8 + [anywhere] * 12,
         out_specs=[vmem] * 6 + [anywhere] * 2,
         scratch_shapes=scratch,
         compiler_params=pltpu.CompilerParams(
             collective_id=collective_id, has_side_effects=True, vmem_limit_bytes=62 * 2**20
         ),
         cost_estimate=pl.CostEstimate(flops=0, bytes_accessed=2**29, transcendentals=0),
-    )(scale, rest, *factors, embedded, noisy, w_in, *far, *parts, head_part)
+    )(scale, bias_grad, rest, *factors, embedded, noisy, w_in, *far, *parts, head_part)
 
 
 def finish_kernel(line, head_rows, *refs):
@@ -1878,7 +1888,6 @@
         grad_final, grad_head, lse, picks = head_pass(
             final_rows, targets_group.reshape(line, 1, tokens), heads, line, head_rows, length, 3
         )
-        ce_part = jnp.sum(lse) / chips - jnp.sum(picks)
     else:
         targets_group = targets_group.reshape(-1)
         handed = lax.ppermute(final_rows[:half], "section", [(1, 0), (0, 1)])
@@ -1910,13 +1919,14 @@
             grad_final, block_out, out_gain[None, :], scale, kept, stacked
         )
         returned = lax.ppermute(grad_second, "section", swapped)
+        lse, picks, out_part = lax.optimization_barrier((lse, picks, out_part))
+        ce_part = jnp.sum(lse) / chips - jnp.sum(picks)
         out_part = out_part.reshape(-1)
         x, joined, mixed, middle, entry_attn, entry_mlp, slope, hidden = kept
         grad_middle, grad_entry, grad_bias, down_part, up_part = backward_begin(
             returned, grad_top, seqs, hidden, entry_mlp, slope, w_up, w_down
         )
         parts = [by_owner(down_part), by_owner(up_part)]
-        grad_bias = grad_bias.reshape(-1)
     else:
         grad_final = grad_final.astype(f32).reshape(stream0.shape)
         out_part = jnp.sum(grad_final * final_normed, (0, 1))
@@ -1941,8 +1951,8 @@
     cond_rows = seqs * 2 * model_width // emb_width
     bias_rows = b_hidden.shape[1] // emb_width
     if straight:
-        rest = jnp.concatenate([grad_bias.reshape(-1, emb_width)] + both, 0).astype(f32)
-        rest = jnp.pad(rest, ((0, -(cond_rows + rest.shape[0]) % 16), (0, 0)))
+        rest = jnp.concatenate(both, 0).astype(f32)
+        rest = jnp.pad(rest, ((0, -(cond_rows + bias_rows + rest.shape[0]) % 16), (0, 0)))
         factors = [
             (value * noise_scale).reshape(tokens, 1) for value in (unit_factor, cubed)
         ]
@@ -1951,6 +1961,7 @@
         far = [grad_middle, grad_entry, middle, x, joined, mixed, entry_attn, w_out, w_qkv]
         grad_down, grad_up, grad_qkv, grad_wout, grad_w_in, grad_head, smalls, rows_all = tail_pass(
             scale,
+            grad_bias,
             rest,
             factors,
             embedded.reshape(tokens, emb_width),

time: 493 us -> 490 us (level)
    ppermute x1, waiting for transfers between devices: 5.74 us -> 0.01 us  [local(): returned = lax.ppermute(grad_second, 'section', swapped)]
where the time goes in v1:
time: 490 us; the launch traced here: 483 us
  Pallas kernels  447 us (91%)
  local copies, waits for them, and re-layouts  14 us (3%)
  other arithmetic  9.06 us (2%)
    pallas_call x1, Pallas kernels, tail_pass(): pl.pallas_call(partial(tail_kernel, line, seqs, line), out_shape=[jax.Sha...  161 us
    pallas_call x1, Pallas kernels, head_pass(): pl.pallas_call(partial(head_kernel, line, head_rows, length), out_shape=[...  129 us
    pallas_call x1, Pallas kernels, forward_pass(): pl.pallas_call(partial(forward_kernel, seqs), out_shape=[jax.ShapeDtypeSt...  47.3 us
    pallas_call x1, Pallas kernels, start_pass(): pl.pallas_call(partial(start_kernel, line), out_shape=[jax.ShapeDtypeStru...  42.2 us
    pallas_call x1, Pallas kernels, backward_pass(): pl.pallas_call(partial(backward_kernel, False, scale.shape[0]), out_shape...  31.4 us
    pallas_call x1, Pallas kernels, backward_begin(): pl.pallas_call(partial(backward_kernel, True, seqs), out_shape=[jax.Shape...  25.9 us
    pallas_call x1, Pallas kernels, finish(): pl.pallas_call(partial(finish_kernel, line, head_rows), out_shape=[jax.Sh...  10.6 us
  transfers between devices with their start and end apart: 2, of which 1 were waited for; matrix products, arithmetic and copies ran while one was open for 1% of the time, Pallas kernels for 0%

profile of v1, /device:TPU:0, one launch (start us, length us, event | category | flops | bytes accessed | tf_op | source)
XLA Modules:
  0.0 482.7 jit_solution(5607880556434996959)
XLA Ops:
  0.7 0.8 reshape.189
  1.5 0.8 reshape.188
  3.6 3.1 pad.25.refs_2_.refs_8_
  6.6 42.2 %shard_map.247 = (s32[4,2,2,8,256]{4,3,2,1,0:T(8,128)}, bf16[2,256,192]{2,1,0:T(8,128)(2,1)}, bf16[640,1024]{1,0:T(8,128)(2,1)}, bf16[1024,1024]{1,0:T(8,128)(2,1)}) custom-call(s32[8,256]{1,0:T(8,128)} %pad.24.refs_0_, bf16[2000,256]{1,0:T(8,128)(2,1)} %refs_1_.1, bf16[1024,1024]{1,0:T(8,128)(2,1)} %pad.25.refs_2_.refs_8_), custom_call_target="tpu_custom_call" | custom-call | bytes 134217728 | tf_op jit(solution)/shard_map/pallas_call | solution.py:187
  48.9 1.1 convert_bitcast_fusion
  49.9 1.0 multiply_reduce_fusion
  53.0 0.7 reshape.206.refs_1_
  53.8 1.5 fusion.1
  55.4 47.3 %shard_map.248 = (bf16[384,1024]{1,0:T(8,128)(2,1)}, bf16[384,1024]{1,0:T(8,128)(2,1)}, f32[384,1024]{1,0:T(8,128)}, bf16[384,3072]{1,0:T(8,128)(2,1)}, bf16[384...) custom-call(f32[384,1024]{1,0:T(8,128)} %bitcast.55, ...), custom_call_target="tpu_custom_call" | custom-call | flops 38654705664 | bytes 33554432 | tf_op jit(solution)/shard_map/pallas_call | solution.py:872
  102.7 128.9 %shard_map.249 = (bf16[384,1024]{1,0:T(8,128)(2,1)}, bf16[4096,1024]{1,0:T(8,128)(2,1)}, f32[4,1,384]{2,1,0:T(1,128)}, f32[4,1,384]{2,1,0:T(1,128)}) custom-call(bf16[384,1024]{1,0:T(8,128)(2,1)} %get-tuple-element.59.refs_0_, s32[4,1,384]{2,1,0:T(1,128)} %reshape.206.refs_1_, bf16[1024,1024]{1,0:T(8,128)(2,1)} %pad.25.refs_2_.refs_8_, ...), custom_call_target="tpu_custom_call" | custom-call | flops 38654705664 | bytes 268435456 | tf_op jit(solution)/shard_map/pallas_call | solution.py:620
  231.6 31.4 %shard_map.250 = (bf16[384,1024]{1,0:T(8,128)(2,1)}, f32[384,1024]{1,0:T(8,128)}, f32[1,1024]{1,0:T(1,128)}) custom-call(f32[3,1,2048]{2,1,0:T(1,128)} %broadcast_in_dim.72.refs_1_.refs_0_, bf16[384,1024]{1,0:T(8,128)(2,1)} %get-tuple-element.64.refs_1_, bf16[384,1024]{1,0:T(8,128)(2,1)} %get-tuple-element.65.refs_2_, f32[1,1024]{1,0:T(1,128)} %bitcast.70, ...), custom_call_target="tpu_custom_call" | custom-call | flops 19327352832 | bytes 33554432 | tf_op jit(solution)/shard_map/pallas_call | solution.py:1084
  265.8 2.7 collective-permute-start.1
  269.5 0.7 multiply_multiply_fusion.refs_4_
  270.5 0.8 copy.66.refs_3_
  271.6 0.8 copy.67.refs_6_
  272.4 0.7 reshape_reshape.11.refs_0_
  273.1 2.2 collective-permute-done.1
  276.0 0.9 copy-done.11
  276.8 25.9 %shard_map.251 = (f32[384,1024]{1,0:T(8,128)}, f32[384,1024]{1,0:T(8,128)}, f32[1,4096]{1,0:T(1,128)}, bf16[4096,1024]{1,0:T(8,128)(2,1)}, bf16[1024,4096]{1,0:T(8,128)(2,1)}) custom-call(bf16[384,1024]{1,0:T(8,128)(2,1)} %copy-done.11, f32[384,1024]{1,0:T(8,128)} %get-tuple-element.71.refs_1_, bf16[384,4096]{1,0:T(8,128)(2,1)} %get-tuple-element.72.refs_2_, ...), custom_call_target="tpu_custom_call" | custom-call | flops 25769803776 | bytes 33554432 | tf_op jit(solution)/shard_map/pallas_call | solution.py:1107
  302.8 160.6 %shard_map.252 = (bf16[256,1024]{1,0:T(8,128)(2,1)}, bf16[64,4096]{1,0:T(8,128)(2,1)}, bf16[64,3072]{1,0:T(8,128)(2,1)}, bf16[64,1024]{1,0:T(8,128)(2,1)}, f32[8...) custom-call(f32[3,1,2048]{2,1,0:T(1,128)} %broadcast_in_dim.72.refs_, ...), custom_call_target="tpu_custom_call" | custom-call | bytes 536870912 | tf_op jit(solution)/shard_map/pallas_call | solution.py:1580
  463.4 1.1 bitcast_convert_fusion
  465.3 0.9 slice.36
  468.9 1.0 convolution_bitcast_fusion
  469.9 10.6 %shard_map.253 = (f32[256,1024]{1,0:T(8,128)}, f32[64,4096]{1,0:T(8,128)}, f32[64,3072]{1,0:T(8,128)}, f32[64,1024]{1,0:T(8,128)}, f32[1000,1024]{1,0:T(8,128)}, /*index=5*/f32[1000,256]{1,0:T(8,128)}) custom-call(s32[1,6144]{1,0:T(1,128)} %reshape_reshape.11.refs_0_, bf16[6144,256]{1,0:T(8,128)(2,1)} %bitcast.68, ...), custom_call_target="tpu_custom_call" | custom-call | flops 3145728000 | bytes 16777216 | tf_op jit(solution)/shard_map/pallas_call | solution.py:1628
  (76 shorter events, 10.2 us)
Async XLA Ops:
  0.6 50.7 %copy-start = (bf16[1,256,2048]{2,1,0:T(8,128)(2,1)S(1)}, bf16[1,256,2048]{2,1,0:T(8,128)(2,1)}, u32[]{:S(2)}) copy-start(bf16[1,256,2048]{2,1,0:T(8,128)(2,1)} %param.23) | copy-start | bytes 3145732
  6.6 44.4 %copy-start.10 = (s32[3]{0:T(128)S(1)}, s32[3]{0:T(128)}, u32[]{:S(2)}) copy-start(s32[3]{0:T(128)} %param.18) | copy-start | bytes 40
  6.6 44.4 %copy-start.12 = (f32[128]{0:T(128)S(1)}, f32[128]{0:T(128)}, u32[]{:S(2)}) copy-start(f32[128]{0:T(128)} %param.19) | copy-start | bytes 1540
  6.6 44.7 %copy-start.7 = (f32[1,2048]{1,0:T(1,128)S(1)}, f32[1,2048]{1,0:T(1,128)}, u32[]{:S(2)}) copy-start(f32[1,2048]{1,0:T(1,128)} %param.24) | copy-start | bytes 24580
  48.8 3.9 copy-start.5
  48.8 4.9 %copy-start.4 = (f32[3,128,256]{2,1,0:T(8,128)S(1)}, f32[3,128,256]{2,1,0:T(8,128)}, u32[]{:S(2)}) copy-start(f32[3,128,256]{2,1,0:T(8,128)} %param.20) | copy-start | bytes 1179652
  48.8 5.0 %copy-start.3 = (bf16[256,1024]{1,0:T(8,128)(2,1)S(1)}, bf16[256,1024]{1,0:T(8,128)(2,1)}, u32[]{:S(2)}) copy-start(bf16[256,1024]{1,0:T(8,128)(2,1)} %refs_7_.3) | copy-start | bytes 1572868
  52.6 50.0 %copy-start.2 = (f32[2,192,256]{2,1,0:T(8,128)}, f32[2,192,256]{2,1,0:T(8,128)S(1)}, u32[]{:S(2)}) copy-start(f32[2,192,256]{2,1,0:T(8,128)S(1)} %copy.58) | copy-start | bytes 1179652
  231.6 31.5 %copy-start.9 = (f32[4,1,384]{2,1,0:T(1,128)S(1)}, f32[4,1,384]{2,1,0:T(1,128)}, u32[]{:S(2)}) copy-start(f32[4,1,384]{2,1,0:T(1,128)} %get-tuple-element.79) | copy-start | bytes 18436
  231.6 32.1 %copy-start.8 = (f32[4,1,384]{2,1,0:T(1,128)S(1)}, f32[4,1,384]{2,1,0:T(1,128)}, u32[]{:S(2)}) copy-start(f32[4,1,384]{2,1,0:T(1,128)} %get-tuple-element.80) | copy-start | bytes 18436
  263.0 13.0 %collective-permute-start = (bf16[384,1024]{1,0:T(8,128)(2,1)}, bf16[384,1024]{1,0:T(8,128)(2,1)S(1)}, u32[]{:S(2)}, u32[]{:S(2)}) collective-permute-start(bf16[384,1024]{1,0:T(8,128)(2,1)} %get-tuple-element.70), channel_id=1, source_target_pairs={{0,16},{16,0},{1,17},{17,1},{2,18},{18,2},{3,19},{19,3},{4,20},{20... | collective-permute-start | bytes 2359304 | tf_op jit(solution)/shard_map/ppermute | solution.py:1921
  265.8 9.5 %collective-permute-start.1 = (bf16[5,256]{1,0:T(8,128)(2,1)S(1)}, bf16[5,256]{1,0:T(8,128)(2,1)S(1)}, u32[]{:S(2)}, u32[]{:S(2)}) collective-permute-start(bf16[5,256]{1,0:T(8,128)(2,1)S(1)} %convert_element_type.43), channel_id=1, source_target_pairs={{0,16},{16,0},{1,17},{17,1},{2,18},{18,2},{3,19},{19,3},{4,20},{20... | collective-permute-start | bytes 7688 | tf_op jit(solution)/shard_map/ppermute | solution.py:1948
  276.0 0.9 copy-start.11
  469.9 10.6 %copy-start.6 = (f32[8,1024]{1,0:T(8,128)S(1)}, f32[8,1024]{1,0:T(8,128)}, u32[]{:S(2)}) copy-start(f32[8,1024]{1,0:T(8,128)} %get-tuple-element.127) | copy-start | bytes 98308
  469.9 11.2 %copy-start.1 = (bf16[1,256,2048]{2,1,0:T(8,128)(2,1)S(1)}, bf16[1,256,2048]{2,1,0:T(8,128)(2,1)}, u32[]{:S(2)}) copy-start(bf16[1,256,2048]{2,1,0:T(8,128)(2,1)} %param.23) | copy-start | bytes 3145732

commit v2 on v1

--- a/solution.py
+++ b/solution.py
@@ -85,6 +85,7 @@
     )
     to_section.start()
     to_other_core = remote(head, head_core, head_send.at[1], head_recv.at[1], core_peer)
+    to_other_core.start()
     place = all_ids.at[me_line, me_pair, me_core]
     copies = [remote(ids, place, ids_send.at[n], ids_recv.at[n], peer) for n, peer in enumerate(peers)]
     for copy in copies:
@@ -156,7 +157,6 @@
         from_core[1, spot] = from_core[1, spot] + own[1, spot] + from_pair[spot]
         if step:
             line_copy(step).start()
-    to_other_core.start()
     total = from_core[1, me_line]
     for step in range(1, line):
         line_copy(step).wait_recv()
@@ -189,7 +189,7 @@
         out_shape=[
             jax.ShapeDtypeStruct((line, 2, 2) + ids.shape, ids.dtype),
             jax.ShapeDtypeStruct((2,) + block, bf16),
-            jax.ShapeDtypeStruct((head.shape[0] // 8 * 5, head.shape[1]), bf16),
+            jax.ShapeDtypeStruct((head.shape[0] // 16 * 7, head.shape[1]), bf16),
             jax.ShapeDtypeStruct(head.shape, bf16),
         ],
         in_specs=[vmem, vmem, anywhere],

time: 490 us -> 496 us (1.012)
  Pallas kernels: 447 us -> 452 us
where the time goes in v2:
time: 496 us; the launch traced here: 489 us
  Pallas kernels  452 us (91%)
  local copies, waits for them, and re-layouts  14 us (3%)
  other arithmetic  9.06 us (2%)
    pallas_call x1, Pallas kernels, tail_pass(): pl.pallas_call(partial(tail_kernel, line, seqs, line), out_shape=[jax.Sha...  162 us
    pallas_call x1, Pallas kernels, head_pass(): pl.pallas_call(partial(head_kernel, line, head_rows, length), out_shape=[...  130 us
    pallas_call x1, Pallas kernels, forward_pass(): pl.pallas_call(partial(forward_kernel, seqs), out_shape=[jax.ShapeDtypeSt...  50.3 us
    pallas_call x1, Pallas kernels, start_pass(): pl.pallas_call(partial(start_kernel, line), out_shape=[jax.ShapeDtypeStru...  41.7 us
    pallas_call x1, Pallas kernels, backward_pass(): pl.pallas_call(partial(backward_kernel, False, scale.shape[0]), out_shape...  31.4 us
    pallas_call x1, Pallas kernels, backward_begin(): pl.pallas_call(partial(backward_kernel, True, seqs), out_shape=[jax.Shape...  25.9 us
    pallas_call x1, Pallas kernels, finish(): pl.pallas_call(partial(finish_kernel, line, head_rows), out_shape=[jax.Sh...  10.6 us
  transfers between devices with their start and end apart: 2, of which 1 were waited for; matrix products, arithmetic and copies ran while one was open for 1% of the time, Pallas kernels for 0%

profile of v2, /device:TPU:0, one launch (start us, length us, event | category | flops | bytes accessed | tf_op | source)
XLA Modules:
  0.0 489.2 jit_solution(8265563552188750480)
XLA Ops:
  0.7 0.8 reshape.189
  1.5 0.8 reshape.188
  3.6 3.1 pad.25.refs_2_.refs_8_
  6.6 41.7 %shard_map.247 = (s32[4,2,2,8,256]{4,3,2,1,0:T(8,128)}, bf16[2,256,192]{2,1,0:T(8,128)(2,1)}, bf16[448,1024]{1,0:T(8,128)(2,1)}, bf16[1024,1024]{1,0:T(8,128)(2,1)}) custom-call(s32[8,256]{1,0:T(8,128)} %pad.24.refs_0_, bf16[2000,256]{1,0:T(8,128)(2,1)} %refs_1_.1, bf16[1024,1024]{1,0:T(8,128)(2,1)} %pad.25.refs_2_.refs_8_), custom_call_target="tpu_custom_call" | custom-call | bytes 134217728 | tf_op jit(solution)/shard_map/pallas_call | solution.py:187
  48.4 1.1 convert_bitcast_fusion
  49.5 1.0 multiply_reduce_fusion
  52.6 0.7 reshape.206.refs_1_
  53.4 1.5 fusion.1
  54.9 50.3 %shard_map.248 = (bf16[384,1024]{1,0:T(8,128)(2,1)}, bf16[384,1024]{1,0:T(8,128)(2,1)}, f32[384,1024]{1,0:T(8,128)}, bf16[384,3072]{1,0:T(8,128)(2,1)}, bf16[384...) custom-call(f32[384,1024]{1,0:T(8,128)} %bitcast.55, ...), custom_call_target="tpu_custom_call" | custom-call | flops 38654705664 | bytes 33554432 | tf_op jit(solution)/shard_map/pallas_call | solution.py:872
  105.3 130.5 %shard_map.249 = (bf16[384,1024]{1,0:T(8,128)(2,1)}, bf16[4096,1024]{1,0:T(8,128)(2,1)}, f32[4,1,384]{2,1,0:T(1,128)}, f32[4,1,384]{2,1,0:T(1,128)}) custom-call(bf16[384,1024]{1,0:T(8,128)(2,1)} %get-tuple-element.59.refs_0_, s32[4,1,384]{2,1,0:T(1,128)} %reshape.206.refs_1_, bf16[1024,1024]{1,0:T(8,128)(2,1)} %pad.25.refs_2_.refs_8_, ...), custom_call_target="tpu_custom_call" | custom-call | flops 38654705664 | bytes 268435456 | tf_op jit(solution)/shard_map/pallas_call | solution.py:620
  235.8 31.4 %shard_map.250 = (bf16[384,1024]{1,0:T(8,128)(2,1)}, f32[384,1024]{1,0:T(8,128)}, f32[1,1024]{1,0:T(1,128)}) custom-call(f32[3,1,2048]{2,1,0:T(1,128)} %broadcast_in_dim.72.refs_1_.refs_0_, bf16[384,1024]{1,0:T(8,128)(2,1)} %get-tuple-element.64.refs_1_, bf16[384,1024]{1,0:T(8,128)(2,1)} %get-tuple-element.65.refs_2_, f32[1,1024]{1,0:T(1,128)} %bitcast.70, ...), custom_call_target="tpu_custom_call" | custom-call | flops 19327352832 | bytes 33554432 | tf_op jit(solution)/shard_map/pallas_call | solution.py:1084
  270.0 2.7 collective-permute-start.1
  273.6 0.7 multiply_multiply_fusion.refs_4_
  274.7 0.8 copy.66.refs_3_
  275.7 0.8 copy.67.refs_6_
  276.6 0.7 reshape_reshape.11.refs_0_
  277.3 3.4 collective-permute-done.1
  281.2 0.9 copy-done.11
  282.1 25.9 %shard_map.251 = (f32[384,1024]{1,0:T(8,128)}, f32[384,1024]{1,0:T(8,128)}, f32[1,4096]{1,0:T(1,128)}, bf16[4096,1024]{1,0:T(8,128)(2,1)}, bf16[1024,4096]{1,0:T(8,128)(2,1)}) custom-call(bf16[384,1024]{1,0:T(8,128)(2,1)} %copy-done.11, f32[384,1024]{1,0:T(8,128)} %get-tuple-element.71.refs_1_, bf16[384,4096]{1,0:T(8,128)(2,1)} %get-tuple-element.72.refs_2_, ...), custom_call_target="tpu_custom_call" | custom-call | flops 25769803776 | bytes 33554432 | tf_op jit(solution)/shard_map/pallas_call | solution.py:1107
  308.0 161.8 %shard_map.252 = (bf16[256,1024]{1,0:T(8,128)(2,1)}, bf16[64,4096]{1,0:T(8,128)(2,1)}, bf16[64,3072]{1,0:T(8,128)(2,1)}, bf16[64,1024]{1,0:T(8,128)(2,1)}, f32[8...) custom-call(f32[3,1,2048]{2,1,0:T(1,128)} %broadcast_in_dim.72.refs_, ...), custom_call_target="tpu_custom_call" | custom-call | bytes 536870912 | tf_op jit(solution)/shard_map/pallas_call | solution.py:1580
  469.8 1.1 bitcast_convert_fusion
  471.7 0.9 slice.36
  475.3 1.0 convolution_bitcast_fusion
  476.4 10.6 %shard_map.253 = (f32[256,1024]{1,0:T(8,128)}, f32[64,4096]{1,0:T(8,128)}, f32[64,3072]{1,0:T(8,128)}, f32[64,1024]{1,0:T(8,128)}, f32[1000,1024]{1,0:T(8,128)}, /*index=5*/f32[1000,256]{1,0:T(8,128)}) custom-call(s32[1,6144]{1,0:T(1,128)} %reshape_reshape.11.refs_0_, bf16[6144,256]{1,0:T(8,128)(2,1)} %bitcast.68, ...), custom_call_target="tpu_custom_call" | custom-call | flops 3145728000 | bytes 16777216 | tf_op jit(solution)/shard_map/pallas_call | solution.py:1628
  (76 shorter events, 10.2 us)
Async XLA Ops:
  0.6 50.2 %copy-start = (bf16[1,256,2048]{2,1,0:T(8,128)(2,1)S(1)}, bf16[1,256,2048]{2,1,0:T(8,128)(2,1)}, u32[]{:S(2)}) copy-start(bf16[1,256,2048]{2,1,0:T(8,128)(2,1)} %param.23) | copy-start | bytes 3145732
  6.6 43.9 %copy-start.10 = (s32[3]{0:T(128)S(1)}, s32[3]{0:T(128)}, u32[]{:S(2)}) copy-start(s32[3]{0:T(128)} %param.18) | copy-start | bytes 40
  6.6 43.9 %copy-start.12 = (f32[128]{0:T(128)S(1)}, f32[128]{0:T(128)}, u32[]{:S(2)}) copy-start(f32[128]{0:T(128)} %param.19) | copy-start | bytes 1540
  6.6 44.2 %copy-start.7 = (f32[1,2048]{1,0:T(1,128)S(1)}, f32[1,2048]{1,0:T(1,128)}, u32[]{:S(2)}) copy-start(f32[1,2048]{1,0:T(1,128)} %param.24) | copy-start | bytes 24580
  48.4 3.9 copy-start.5
  48.4 4.9 copy-start.4
  48.4 5.0 %copy-start.3 = (bf16[256,1024]{1,0:T(8,128)(2,1)S(1)}, bf16[256,1024]{1,0:T(8,128)(2,1)}, u32[]{:S(2)}) copy-start(bf16[256,1024]{1,0:T(8,128)(2,1)} %refs_7_.3) | copy-start | bytes 1572868
  52.2 53.1 %copy-start.2 = (f32[2,192,256]{2,1,0:T(8,128)}, f32[2,192,256]{2,1,0:T(8,128)S(1)}, u32[]{:S(2)}) copy-start(f32[2,192,256]{2,1,0:T(8,128)S(1)} %copy.58) | copy-start | bytes 1179652
  235.8 31.5 %copy-start.9 = (f32[4,1,384]{2,1,0:T(1,128)S(1)}, f32[4,1,384]{2,1,0:T(1,128)}, u32[]{:S(2)}) copy-start(f32[4,1,384]{2,1,0:T(1,128)} %get-tuple-element.79) | copy-start | bytes 18436
  235.8 32.1 %copy-start.8 = (f32[4,1,384]{2,1,0:T(1,128)S(1)}, f32[4,1,384]{2,1,0:T(1,128)}, u32[]{:S(2)}) copy-start(f32[4,1,384]{2,1,0:T(1,128)} %get-tuple-element.80) | copy-start | bytes 18436
  267.2 14.1 %collective-permute-start = (bf16[384,1024]{1,0:T(8,128)(2,1)}, bf16[384,1024]{1,0:T(8,128)(2,1)S(1)}, u32[]{:S(2)}, u32[]{:S(2)}) collective-permute-start(bf16[384,1024]{1,0:T(8,128)(2,1)} %get-tuple-element.70), channel_id=1, source_target_pairs={{0,16},{16,0},{1,17},{17,1},{2,18},{18,2},{3,19},{19,3},{4,20},{20... | collective-permute-start | bytes 2359304 | tf_op jit(solution)/shard_map/ppermute | solution.py:1921
  270.0 10.6 %collective-permute-start.1 = (bf16[5,256]{1,0:T(8,128)(2,1)S(1)}, bf16[5,256]{1,0:T(8,128)(2,1)S(1)}, u32[]{:S(2)}, u32[]{:S(2)}) collective-permute-start(bf16[5,256]{1,0:T(8,128)(2,1)S(1)} %convert_element_type.43), channel_id=1, source_target_pairs={{0,16},{16,0},{1,17},{17,1},{2,18},{18,2},{3,19},{19,3},{4,20},{20... | collective-permute-start | bytes 7688 | tf_op jit(solution)/shard_map/ppermute | solution.py:1948
  281.2 0.9 copy-start.11
  476.4 10.6 %copy-start.6 = (f32[8,1024]{1,0:T(8,128)S(1)}, f32[8,1024]{1,0:T(8,128)}, u32[]{:S(2)}) copy-start(f32[8,1024]{1,0:T(8,128)} %get-tuple-element.127) | copy-start | bytes 98308
  476.4 11.2 %copy-start.1 = (bf16[1,256,2048]{2,1,0:T(8,128)(2,1)S(1)}, bf16[1,256,2048]{2,1,0:T(8,128)(2,1)}, u32[]{:S(2)}) copy-start(bf16[1,256,2048]{2,1,0:T(8,128)(2,1)} %param.23) | copy-start | bytes 3145732
